TPU v7x, 256 devices: a whole 4x4x8 slice. The times are simulated.
256 devices in a mesh: mz: 32 (over z, y), rt: 4 (over x), samp: 2 (over core).
Axes of the slice: x: 4, y: 4, z: 8, core: 2. Of those that a mesh axis runs over, the one named last changes fastest.
Arguments:
- spectra: float32 [8, 2048, 16384], P('samp', 'rt', 'mz'), may hold values from -120 to 120
- sample_factor: float32 [32, 8], P(None, 'samp'), may hold values from 0.2 to 1
- scan_factor: float32 [32, 2048], P('mz', 'rt'), may hold values from -0.125 to 0.125
Outputs:
- mz_factor: float32 [32, 16384], P(None, ('mz', 'rt', 'samp'))
- peak_scales: float32 [32], replicated
- factor_gram: float32 [32, 32], replicated
All inputs are finite; a program needn't handle non-finite values. Where the computation divides by a largest or mean magnitude, that divisor is 1e-20 or more.
Results may differ from a plain program's by a relative error of at most 0.00014.
Values sent between devices are 32-bit elements; how exact they have to be, the bound alone decides.
No kernel may reach another device: no remote copies, remote signals or barrier semaphores. Data moves between devices by JAX's collectives and lax.ppermute only.
A program may use at most 64 MiB of HBM per device.

v0:
```python
import jax
import jax.numpy as jnp
from jax import lax
from jax.sharding import PartitionSpec as P

MZ = 16384


def local(spectra, sample_factor, scan_factor):
    highest = lax.Precision.HIGHEST
    samples_all = lax.all_gather(sample_factor, "samp", axis=1, tiled=True)
    scan_block = lax.all_gather(scan_factor, "mz", axis=0, tiled=True)
    gram_sample = jnp.dot(samples_all, samples_all.T, precision=highest)
    gram_scan = lax.psum(jnp.dot(scan_block, scan_block.T, precision=highest), "rt")
    system = gram_sample * gram_scan
    components, sample_count = sample_factor.shape
    scan_count = scan_block.shape[1]
    khatri = (sample_factor[:, :, None] * scan_block[:, None, :]).reshape(
        components, sample_count * scan_count
    )
    partial_sum = jnp.dot(
        khatri, spectra.reshape(sample_count * scan_count, spectra.shape[2]), precision=highest
    )
    owned_rows = lax.psum_scatter(partial_sum, ("rt", "samp"), scatter_dimension=1, tiled=True)
    chol_lower = jnp.linalg.cholesky(system)
    raw_factor = jax.scipy.linalg.cho_solve((chol_lower, True), owned_rows)
    local_peaks = jnp.max(jnp.abs(raw_factor), axis=1)
    peak_values = lax.pmax(local_peaks, ("mz", "rt", "samp")) + 1e-06
    mz_factor = raw_factor / peak_values[:, None]
    factor_gram = (
        lax.psum(jnp.dot(mz_factor, mz_factor.T, precision=highest), ("mz", "rt", "samp")) / MZ
    )
    return (mz_factor, peak_values, factor_gram)


def solution(mesh):
    return jax.shard_map(
        local,
        mesh=mesh,
        in_specs=(P("samp", "rt", "mz"), P(None, "samp"), P("mz", "rt")),
        out_specs=(P(None, ("mz", "rt", "samp")), P(), P()),
        check_vma=False,
    )
```

profile of v0, /device:TPU:1, one launch (start us, length us, event | category | flops | bytes accessed | tf_op | source)
XLA Modules:
  0.0 260.2 jit_solution(15873467965445823029)
XLA Ops:
  7.2 0.0 copy-start.1
  7.2 0.0 reduce-scatter.4.cloned.1.call-start
  7.2 0.8 copy.13
  8.0 40.5 %all-gather.1 = f32[32,1,512]{2,1,0:T(1,128)S(1)} all-gather(f32[1,1,512]{2,1,0:T(1,128)} %bitcast.39), channel_id=1, replica_groups=mesh['mz'=32,'rt'=4,'samp'=2] {'mz'}, dimensions={0}, use_global_device_ids=true | all-gather | bytes 67584 | tf_op jit(solution)/shard_map/all_gather | solution.py:12
  48.5 0.1 broadcast_multiply_fusion
  48.6 9.6 %convolution_bitcast_fusion = f32[512,32]{1,0:T(8,128)} fusion(f32[4,512,512]{2,1,0:T(8,128)} %param.3, f32[32,4,512]{2,1,0:T(4,128)S(1)} %broadcast_multiply_fusion), kind=kOutput, calls=%fused_computation | convolution fusion | flops 402653184 | bytes 4521984 | tf_op jit(solution)/shard_map/dot_general | solution.py:21
  58.2 0.0 reduce-scatter.4.cloned.1.call-update
  58.2 0.2 fusion.8
  58.4 0.0 copy-done.1
  58.5 14.6 %all-gather = f32[2,4,32]{2,1,0:T(4,128)S(1)} all-gather(f32[1,4,32]{2,1,0:T(4,128)S(1)} %bitcast.37), channel_id=1, replica_groups=mesh['mz'=32,'rt'=4,'samp'=2] {'samp'}, dimensions={0}, use_global_device_ids=true | all-gather | bytes 1536 | tf_op jit(solution)/shard_map/all_gather | solution.py:11
  73.0 13.1 %psum.14 = f32[32,32]{0,1:T(8,128)S(1)} all-reduce(f32[32,32]{0,1:T(8,128)S(1)} %fusion.8), channel_id=1, replica_groups=mesh['mz'=32,'rt'=4,'samp'=2] {'rt'}, use_global_device_ids=true, to_apply=%region_0.0 | all-reduce | flops 1024 | bytes 8192 | tf_op jit(solution)/shard_map/psum | solution.py:14
  86.1 0.2 convolution_multiply_fusion
  86.4 0.1 copy.12
  86.4 2.9 %cholesky.16 = f32[32,32]{1,0:T(8,128)S(1)} custom-call(f32[32,32]{1,0:T(8,128)S(1)} %fusion.7), custom_call_target="Cholesky" | custom-call | tf_op jit(solution)/shard_map/jit(cholesky)/cholesky | solution.py:25
  89.4 0.6 compare_reduce_fusion
  90.0 0.7 fusion.3
  90.7 2.4 custom-call.10
  93.1 6.1 %reduce-scatter.4.cloned.1.call-done = f32[64,32]{1,0:T(8,128)} async-done(((f32[512,32]{1,0:T(8,128)}), f32[64,32]{1,0:T(8,128)}) %reduce-scatter.4.cloned.1.call-update) | async-done | bytes 8208
  99.3 1.0 fusion.1
  100.2 0.3 abs_reduce_fusion
  100.5 78.4 %pmax.7 = f32[32]{0:T(128)S(1)} all-reduce(f32[32]{0:T(128)S(1)} %get-tuple-element.3), channel_id=1, replica_groups=mesh['mz'=32,'rt'=4,'samp'=2] {'mz','rt','samp'}, use_global_device_ids=true, to_apply=%region_5.6 | all-reduce | flops 32 | bytes 256 | tf_op jit(solution)/shard_map/pmax | solution.py:28
  178.9 0.0 copy-start.2
  178.9 0.1 broadcast_divide_fusion
  179.0 0.0 copy-start
  179.0 0.1 fusion.9
  179.1 73.6 %psum.15 = f32[32,32]{1,0:T(8,128)S(1)} all-reduce(f32[32,32]{1,0:T(8,128)S(1)} %fusion.9), channel_id=1, replica_groups=mesh['mz'=32,'rt'=4,'samp'=2] {'mz','rt','samp'}, use_global_device_ids=true, to_apply=%region_6.7 | all-reduce | flops 1024 | bytes 8192 | tf_op jit(solution)/shard_map/psum | solution.py:31
  252.7 0.6 broadcast_multiply_fusion.1
  253.3 0.0 copy-done.2
  253.3 0.0 copy-done
  (4 shorter events, 0.0 us)
Async XLA Ops:
  7.2 51.3 %copy-start.1 = (f32[32,4]{0,1:T(4,128)S(1)}, f32[32,4]{0,1:T(4,128)}, u32[]{:S(2)}) copy-start(f32[32,4]{0,1:T(4,128)} %param.4) | copy-start | bytes 1540
  7.2 92.1 %reduce-scatter.4.cloned.1.call-start = ((), (), s32[]{:S(2)}) async-start(), calls=%async_computation.1 | async-start | bytes 294912
  178.9 74.4 %copy-start.2 = (f32[32]{0:T(128)}, f32[32]{0:T(128)S(1)}, u32[]{:S(2)}) copy-start(f32[32]{0:T(128)S(1)} %broadcast_add_fusion) | copy-start | bytes 388
  179.0 74.4 %copy-start = (f32[32,64]{1,0:T(8,128)}, f32[32,64]{1,0:T(8,128)S(1)}, u32[]{:S(2)}) copy-start(f32[32,64]{1,0:T(8,128)S(1)} %broadcast_divide_fusion) | copy-start | bytes 24580
Sparse Core Ops, SparseCore 0:
  58.4 40.8 reduce-scatter.3
where the time goes:
time: 261 us; the launch traced here: 260 us
  blocking collectives  220 us (84%)
  between operations  14.1 us (5%)
  matrix products  11.3 us (4%)
  other arithmetic  7.48 us (3%)
  waiting for transfers between devices  6.15 us (2%)
    pmax x1, blocking collectives, local(): peak_values = lax.pmax(local_peaks, ('mz', 'rt', 'samp')) + 1e-06  78.4 us
    psum x1, blocking collectives, local(): lax.psum(jnp.dot(mz_factor, mz_factor.T, precision=highest), ('mz', 'rt',...  73.6 us
    all_gather x1, blocking collectives, local(): scan_block = lax.all_gather(scan_factor, 'mz', axis=0, tiled=True)  40.5 us
    all_gather x1, blocking collectives, local(): samples_all = lax.all_gather(sample_factor, 'samp', axis=1, tiled=True)  14.6 us
    psum x1, blocking collectives, local(): lax.psum(jnp.dot(scan_block, scan_block.T, precision=highest), 'rt')  13.1 us
    dot_general x1, matrix products, local(): jnp.dot(khatri, spectra.reshape(sample_count * scan_count, spectra.shape[...  9.57 us
    unnamed x2, waiting for transfers between devices  6.15 us
  transfers between devices with their start and end apart: 1, of which 1 were waited for; matrix products, arithmetic and copies ran while one was open for 3% of the time, Pallas kernels for 0%

commit v1 on v0

v1 whole, which is shorter than its diff:
```python
import jax
import jax.numpy as jnp
from jax import lax
from jax.experimental import pallas as pl
from jax.experimental.pallas import tpu as pltpu
from jax.sharding import PartitionSpec as P

MZ = 16384
RANK = 32
HIGHEST = lax.Precision.HIGHEST
F32 = jnp.float32
VMEM = pl.BlockSpec(memory_space=pltpu.VMEM)


def iota(shape, dim):
    return lax.broadcasted_iota(jnp.int32, shape, dim)


def split(x):
    high = x.astype(jnp.bfloat16)
    return high, (x - high.astype(F32)).astype(jnp.bfloat16)


def nt_dot(a, b):
    return lax.dot_general(
        a, b, (((1,), (1,)), ((), ())), precision=HIGHEST, preferred_element_type=F32
    )


def contract_kernel(spectra_ref, sample_ref, scan_ref, keep_ref, send_ref, buffer, sems):
    count = spectra_ref.shape[0]
    copies = [
        pltpu.make_async_copy(spectra_ref.at[s], buffer.at[s], sems.at[s]) for s in range(count)
    ]
    for copy in copies:
        copy.start()
    scan = scan_ref[...]
    sample = sample_ref[...]
    gram = nt_dot(scan, scan)
    scan_high, scan_low = split(scan)
    stacked = jnp.concatenate([scan_high, scan_low], axis=0)
    total = jnp.zeros((RANK, spectra_ref.shape[2]), F32)
    for s in range(count):
        copies[s].wait()
        high, low = split(buffer[s])
        both = jnp.dot(stacked, high, preferred_element_type=F32)
        part = both[:RANK] + both[RANK:] + jnp.dot(scan_high, low, preferred_element_type=F32)
        total = total + sample[:, s : s + 1] * part
    core = lax.axis_index("samp")
    first = iota((RANK, 128), 1) < 64
    halves = ([], [])
    for t in range(0, 4, 2):
        a, b = total[:, t * 128 : (t + 1) * 128], total[:, (t + 1) * 128 : (t + 2) * 128]
        halves[0].append(jnp.where(first, a, pltpu.roll(b, 64, 1)))
        halves[1].append(jnp.where(first, pltpu.roll(a, 64, 1), b))
    for t in range(2):
        cut = slice(t * 128, (t + 1) * 128)
        keep_ref[:, cut] = jnp.where(core == 0, halves[0][t], halves[1][t])
        send_ref[:, cut] = jnp.where(core == 0, halves[1][t], halves[0][t])
    keep_ref[:, 256:] = jnp.zeros((RANK, 128), F32)
    send_ref[:, 256:] = jnp.zeros((RANK, 128), F32)
    keep_ref[:, 256 : 256 + RANK] = gram
    send_ref[:, 256 : 256 + count] = sample


def packed_index(count):
    place = iota((RANK, count), 1)
    whole = place < 512
    row = jnp.where(whole, place >> 5, 16 + ((place - 512) >> 4))
    column = jnp.where(whole, place & 31, 16 + (place & 15))
    return row, column


def solve_kernel(mine_ref, other_ref, sample_ref, sample_other_ref, raw_ref, packet_ref):
    own, away = sample_ref[...], sample_other_ref[:, 256 : 256 + sample_ref.shape[1]]
    system = (nt_dot(own, own) + nt_dot(away, away)) * mine_ref[:, 256 : 256 + RANK]
    parts = [mine_ref[:, :256], other_ref[...]]
    row_of = iota((RANK, 1), 0)
    for k in range(RANK):
        here = row_of == k
        scale = 1.0 / system[k : k + 1, k : k + 1]
        column = jnp.where(here, -1.0, system[:, k : k + 1])
        parts = [
            jnp.where(here, 0.0, part) - column * (part[k : k + 1] * scale) for part in parts
        ]
        system = jnp.where(here, 0.0, system) - column * (system[k : k + 1] * scale)
    slot = lax.axis_index("rt")
    pair = jnp.where(slot < 2, parts[0][:, :128], parts[0][:, 128:])
    raw_ref[...] = jnp.where(slot % 2 == 0, pair, pltpu.roll(pair, 64, 1))[:, :64]
    peak = jnp.maximum(*(jnp.max(jnp.abs(part), axis=1, keepdims=True) for part in parts)) + 1e-06
    scaled = [part / peak for part in parts]
    gram = nt_dot(scaled[0], scaled[0]) + nt_dot(scaled[1], scaled[1])
    row, column = packed_index(768)
    spread = jnp.where(iota((RANK, 768), 0) == column, 1.0, 0.0)
    flat = jnp.dot(gram, spread, precision=HIGHEST, preferred_element_type=F32)
    flat = jnp.sum(jnp.where(iota((RANK, 768), 0) == row, flat, 0.0), axis=0, keepdims=True)
    lane = iota((RANK, 128), 1)
    peak_row = jnp.sum(jnp.where(lane == row_of, peak, 0.0), axis=0, keepdims=True)
    packet = jnp.concatenate(
        [flat[:, u * 128 : (u + 1) * 128] for u in range(6)] + [peak_row, jnp.zeros((1, 128), F32)],
        axis=0,
    )
    for d in range(packet_ref.shape[0]):
        packet_ref[d] = packet


def finish_kernel(packets_ref, raw_ref, factor_ref, peak_ref, gram_ref):
    peaks = packets_ref[:, 6, :RANK]
    peak_row = jnp.max(peaks, axis=0, keepdims=True)
    ratio = peaks / peak_row
    row, column = packed_index(768)
    component = iota((RANK, 768), 0)
    of_row, of_column = component == row, component == column
    row_scale = jnp.dot(
        ratio, jnp.where(of_row, 1.0, 0.0), precision=HIGHEST, preferred_element_type=F32
    )
    column_scale = jnp.dot(
        ratio, jnp.where(of_column, 1.0, 0.0), precision=HIGHEST, preferred_element_type=F32
    )
    packed = jnp.concatenate([packets_ref[:, u, :] for u in range(6)], axis=1)
    flat = jnp.sum(packed * row_scale * column_scale, axis=0, keepdims=True) * (1.0 / MZ)
    gram = nt_dot(jnp.where(of_row, flat, 0.0), jnp.where(of_column, 1.0, 0.0))
    place = iota((RANK, 768), 1)
    corner = (place < 512) & (column >= 16)
    gram = gram + nt_dot(
        jnp.where(of_column & corner, flat, 0.0), jnp.where(of_row & corner, 1.0, 0.0)
    )
    peak_ref[...] = peak_row
    diagonal = iota((RANK, RANK), 0) == iota((RANK, RANK), 1)
    peak = jnp.sum(jnp.where(diagonal, peak_row, 0.0), axis=1, keepdims=True)
    factor_ref[...] = raw_ref[...] / peak
    gram_ref[...] = gram


def call(kernel, shapes, ins, scratch=(), name=None):
    return pl.pallas_call(
        kernel,
        out_shape=[jax.ShapeDtypeStruct(s, F32) for s in shapes],
        in_specs=ins,
        out_specs=[VMEM] * len(shapes),
        scratch_shapes=list(scratch),
        compiler_params=pltpu.CompilerParams(vmem_limit_bytes=32 * 1024 * 1024),
        name=name,
    )


def shift(x, axis, size, by):
    return lax.ppermute(x, axis, [(i, (i + by) % size) for i in range(size)])


def local(spectra, sample_factor, scan_factor):
    bins = spectra.shape[2]
    rows = jnp.broadcast_to(scan_factor[None], (RANK, 1, scan_factor.shape[1]))
    scan_block = lax.all_to_all(rows, "mz", 0, 0).reshape(RANK, scan_factor.shape[1])
    half = bins // 2
    keep, send = call(
        contract_kernel,
        [(RANK, half + 128)] * 2,
        [pl.BlockSpec(memory_space=pl.ANY), VMEM, VMEM],
        [pltpu.VMEM(spectra.shape, F32), pltpu.SemaphoreType.DMA((spectra.shape[0],))],
        "contract",
    )(spectra, sample_factor, scan_block)
    taken = shift(send, "samp", 2, 1)
    lane = iota(keep.shape, 1)
    partial = keep + jnp.where(lane < half, taken, 0.0)
    far = [shift(partial, "rt", 4, by) for by in (1, 2, 3)]
    mine = (partial + far[1]) + (far[0] + far[2])
    other = shift(mine[:, :half], "samp", 2, 1)
    raw, packets = call(
        solve_kernel, [(RANK, 64), (RANK, 8, 128)], [VMEM] * 4, name="solve"
    )(mine, other, sample_factor, taken)
    packets = lax.all_to_all(packets, "mz", 0, 0)
    factor, peak, gram = call(
        finish_kernel, [(RANK, 64), (1, RANK), (RANK, RANK)], [VMEM] * 2, name="finish"
    )(packets, raw)
    return (factor, peak.reshape(RANK), gram)


def solution(mesh):
    return jax.shard_map(
        local,
        mesh=mesh,
        in_specs=(P("samp", "rt", "mz"), P(None, "samp"), P("mz", "rt")),
        out_specs=(P(None, ("mz", "rt", "samp")), P(), P()),
        check_vma=False,
    )
```

time: 261 us -> 58.4 us (0.22)
  blocking collectives: 220 us -> 12.4 us
  starting transfers between devices: 0.04 us -> 20.3 us
  between operations: 14.1 us -> 0.68 us
  matrix products: 11.3 us -> 0 us
  other arithmetic: 7.48 us -> 0.03 us
  Pallas kernels: 0 us -> 6.84 us
  waiting for transfers between devices: 6.15 us -> 12.9 us
  local copies, waits for them, and re-layouts: 0.87 us -> 4.3 us
    psum x2 -> x0, blocking collectives: 86.7 us -> none  [the longest x1 73.6 us: local(): lax.psum(jnp.dot(mz_factor, mz_factor.T, precision=highest), ('mz', 'rt',...]
    pmax x1 -> x0, blocking collectives: 78.4 us -> none  [local(): peak_values = lax.pmax(local_peaks, ('mz', 'rt', 'samp')) + 1e-06]
    all_gather x2 -> x0, blocking collectives: 55.1 us -> none  [the longest x1 40.5 us: local(): scan_block = lax.all_gather(scan_factor, 'mz', axis=0, tiled=True)]
    all_to_all x0 -> x1, blocking collectives: none -> 12.4 us  [local(): packets = lax.all_to_all(packets, 'mz', 0, 0)]
    all_to_all x0 -> x1, starting transfers between devices: none -> 12 us  [local(): lax.all_to_all(rows, 'mz', 0, 0).reshape(RANK, scan_factor.shape[1])]
    dot_general x4 -> x0, matrix products: 10.1 us -> none  [the longest x1 9.57 us: local(): jnp.dot(khatri, spectra.reshape(sample_count * scan_count, spectra.shape[...]
    ppermute x0 -> x5, starting transfers between devices: none -> 8.3 us  [shift(): return lax.ppermute(x, axis, [(i, (i + by) % size) for i in range(size)])]
    all_to_all x0 -> x1, waiting for transfers between devices: none -> 8.05 us  [local(): lax.all_to_all(rows, 'mz', 0, 0).reshape(RANK, scan_factor.shape[1])]
  transfers between devices with their start and end apart: 1 -> 6, of which waited for: 1 -> 5; matrix products, arithmetic and copies ran while one was open for 3% -> 1% of each run, Pallas kernels for 0% -> 0%
where the time goes in v1:
time: 58.4 us; the launch traced here: 57.4 us
  starting transfers between devices  20.3 us (35%)
  waiting for transfers between devices  12.9 us (22%)
  blocking collectives  12.4 us (21%)
  Pallas kernels  6.84 us (12%)
  local copies, waits for them, and re-layouts  4.3 us (7%)
  between operations  0.68 us (1%)
    all_to_all x1, blocking collectives, local(): packets = lax.all_to_all(packets, 'mz', 0, 0)  12.4 us
    all_to_all x1, starting transfers between devices, local(): lax.all_to_all(rows, 'mz', 0, 0).reshape(RANK, scan_factor.shape[1])  12 us
    ppermute x5, starting transfers between devices, shift(): return lax.ppermute(x, axis, [(i, (i + by) % size) for i in range(size)])  8.3 us
    all_to_all x1, waiting for transfers between devices, local(): lax.all_to_all(rows, 'mz', 0, 0).reshape(RANK, scan_factor.shape[1])  8.05 us
    ppermute x5, waiting for transfers between devices, shift(): return lax.ppermute(x, axis, [(i, (i + by) % size) for i in range(size)])  4.84 us
    pallas_call x1, Pallas kernels, local(): call(solve_kernel, [(RANK, 64), (RANK, 8, 128)], [VMEM] * 4, name='solve')  3.41 us
    unnamed x4, local copies, waits for them, and re-layouts  2.96 us
    pallas_call x1, Pallas kernels, local(): call(contract_kernel, [(RANK, half + 128)] * 2, [pl.BlockSpec(memory_spac...  2.21 us
  transfers between devices with their start and end apart: 6, of which 5 were waited for; matrix products, arithmetic and copies ran while one was open for 1% of the time, Pallas kernels for 0%

profile of v1, /device:TPU:1, one launch (start us, length us, event | category | flops | bytes accessed | tf_op | source)
XLA Modules:
  0.0 57.4 jit_solution(11076477107982371504)
XLA Ops:
  0.6 1.3 %broadcast_in_dim.13 = f32[32,1,512]{2,1,0:T(1,128)} broadcast(f32[512]{0:T(512)} %bitcast.6), dimensions={2} | broadcast | bytes 67584 | tf_op jit(solution)/shard_map/broadcast_in_dim | solution.py:153
  2.0 12.0 %all-to-all-start = ((f32[32,1,512]{2,1,0:T(1,128)}), f32[32,1,512]{2,1,0:T(1,128)S(1)}, u32[]{:S(2)}, u32[]{:S(2)}) async-start(f32[32,1,512]{2,1,0:T(1,128)} %broadcast_in_dim.13), calls=%async_computation | async-start | bytes 131072 | tf_op jit(solution)/shard_map/all_to_all | solution.py:154
  14.0 0.8 %copy.8.sample_ref = f32[32,4]{1,0:T(8,128)S(1)} copy(f32[32,4]{0,1:T(4,128)} %param.4) | data formatting | bytes 1024 | tf_op args[1]
  14.8 8.1 %all-to-all-done = f32[32,1,512]{2,1,0:T(1,128)S(1)} async-done(((f32[32,1,512]{2,1,0:T(1,128)}), f32[32,1,512]{2,1,0:T(1,128)S(1)}, u32[]{:S(2)}, u32[]{:S(2)}) %all-to-all-start) | async-done | bytes 65568 | tf_op jit(solution)/shard_map/all_to_all | solution.py:154
  22.8 0.0 copy-start
  22.8 2.2 %copy-done = f32[4,512,512]{2,1,0:T(8,128)S(1)} copy-done((f32[4,512,512]{2,1,0:T(8,128)S(1)}, f32[4,512,512]{2,1,0:T(8,128)}, u32[]{:S(2)}) %copy-start) | copy-done | bytes 4194328
  25.0 2.2 %contract.1 = (f32[32,384]{1,0:T(8,128)S(1)}, f32[32,384]{1,0:T(8,128)S(1)}) custom-call(f32[4,512,512]{2,1,0:T(8,128)S(1)} %copy-done, f32[32,4]{1,0:T(8,128)S(1)} %copy.8.sample_ref, f32[32,512]{1,0:T(8,128)S(1)} %bitcast.5), custom_call_target="tpu_custom_call" | custom-call | tf_op jit(solution)/shard_map/contract/pallas_call | solution.py:156
  27.2 2.2 %collective-permute-start = (f32[32,384]{1,0:T(8,128)S(1)}, f32[32,384]{1,0:T(8,128)S(1)}, u32[]{:S(2)}, u32[]{:S(2)}) collective-permute-start(f32[32,384]{1,0:T(8,128)S(1)} %get-tuple-element.11), channel_id=1, source_target_pairs={{0,1},{1,0},{2,3},{3,2},{4,5},{5,4},{6,7},{7,6},{8,9},{9,8},{10,11... | collective-permute-start | bytes 147464 | tf_op jit(solution)/shard_map/ppermute | solution.py:148
  29.4 0.9 %collective-permute-done.sample_other_ref = f32[32,384]{1,0:T(8,128)S(1)} collective-permute-done((f32[32,384]{1,0:T(8,128)S(1)}, f32[32,384]{1,0:T(8,128)S(1)}, u32[]{:S(2)}, u32[]{:S(2)}) %collective-permute-start) | collective-permute-done | bytes 49184 | tf_op jit(solution)/shard_map/ppermute | solution.py:148
  30.3 2.6 %collective-permute-start.3 = (f32[32,384]{1,0:T(8,128)S(1)}, f32[32,384]{1,0:T(8,128)S(1)}, u32[]{:S(2)}, u32[]{:S(2)}) collective-permute-start(f32[32,384]{1,0:T(8,128)S(1)} %select_add_fusion), channel_id=1, source_target_pairs={{0,6},{2,0},{4,2},{6,4},{1,7},{3,1},{5,3},{7,5},{8,14},{10,8},{12,... | collective-permute-start | bytes 147464 | tf_op jit(solution)/shard_map/ppermute | solution.py:148
  32.9 0.0 collective-permute-start.2
  32.9 1.7 %collective-permute-start.1 = (f32[32,384]{1,0:T(8,128)S(1)}, f32[32,384]{1,0:T(8,128)S(1)}, u32[]{:S(2)}, u32[]{:S(2)}) collective-permute-start(f32[32,384]{1,0:T(8,128)S(1)} %select_add_fusion), channel_id=1, source_target_pairs={{0,4},{2,6},{4,0},{6,2},{1,5},{3,7},{5,1},{7,3},{8,12},{10,14},{12... | collective-permute-start | bytes 147464 | tf_op jit(solution)/shard_map/ppermute | solution.py:148
  34.6 0.0 collective-permute-done.3
  34.6 2.6 %collective-permute-done.2 = f32[32,384]{1,0:T(8,128)S(1)} collective-permute-done((f32[32,384]{1,0:T(8,128)S(1)}, f32[32,384]{1,0:T(8,128)S(1)}, u32[]{:S(2)}, u32[]{:S(2)}) %collective-permute-start.2) | collective-permute-done | bytes 49184 | tf_op jit(solution)/shard_map/ppermute | solution.py:148
  37.3 0.5 collective-permute-done.1
  37.7 1.8 %collective-permute-start.4 = (f32[32,256]{1,0:T(8,128)S(1)}, f32[32,256]{1,0:T(8,128)S(1)}, u32[]{:S(2)}, u32[]{:S(2)}) collective-permute-start(f32[32,256]{1,0:T(8,128)S(1)} %slice.4), channel_id=1, source_target_pairs={{0,1},{1,0},{2,3},{3,2},{4,5},{5,4},{6,7},{7,6},{8,9},{9,8},{10,11... | collective-permute-start | bytes 98312 | tf_op jit(solution)/shard_map/ppermute | solution.py:148
  39.6 0.9 %collective-permute-done.4.other_ref = f32[32,256]{1,0:T(8,128)S(1)} collective-permute-done((f32[32,256]{1,0:T(8,128)S(1)}, f32[32,256]{1,0:T(8,128)S(1)}, u32[]{:S(2)}, u32[]{:S(2)}) %collective-permute-start.4) | collective-permute-done | bytes 32800 | tf_op jit(solution)/shard_map/ppermute | solution.py:148
  40.4 3.4 %solve.1 = (f32[32,64]{1,0:T(8,128)S(1)}, f32[32,8,128]{2,1,0:T(8,128)S(1)}) custom-call(f32[32,384]{1,0:T(8,128)S(1)} %add_add_fusion.mine_ref, f32[32,256]{1,0:T(8,128)S(1)} %collective-permute-done.4.other_ref, f32[32,4]{1,0:T(8,128)S(1)} %copy.8.sample_ref, f32[32,384]{1,0:T(8,128)S(1)} %collective-permute-done.sample_other_ref), custom_call_target="tpu_custom_call" | custom-call | tf_op jit(solution)/shard_map/solve/pallas_call | solution.py:169
  43.9 12.4 %all_to_all.10.packets_ref = f32[32,8,128]{2,1,0:T(8,128)S(1)} all-to-all(f32[32,8,128]{2,1,0:T(8,128)S(1)} %get-tuple-element.12), channel_id=1, replica_groups=mesh['mz'=32,'rt'=4,'samp'=2] {'mz'}, dimensions={0} | all-to-all | bytes 262144 | tf_op jit(solution)/shard_map/all_to_all | solution.py:172
  56.2 1.2 %finish.1 = (f32[32,64]{1,0:T(8,128)}, f32[1,32]{1,0:T(1,128)}, f32[32,32]{1,0:T(8,128)}) custom-call(f32[32,8,128]{2,1,0:T(8,128)S(1)} %all_to_all.10.packets_ref, f32[32,64]{1,0:T(8,128)S(1)} %get-tuple-element.13.raw_ref), custom_call_target="tpu_custom_call" | custom-call | tf_op jit(solution)/shard_map/finish/pallas_call | solution.py:173
  (5 shorter events, 0.0 us)
Async XLA Ops:
  2.0 20.9 %all-to-all-start = ((f32[32,1,512]{2,1,0:T(1,128)}), f32[32,1,512]{2,1,0:T(1,128)S(1)}, u32[]{:S(2)}, u32[]{:S(2)}) async-start(f32[32,1,512]{2,1,0:T(1,128)} %broadcast_in_dim.13), calls=%async_computation | async-start | bytes 131072 | tf_op jit(solution)/shard_map/all_to_all | solution.py:154
  22.8 2.2 %copy-start = (f32[4,512,512]{2,1,0:T(8,128)S(1)}, f32[4,512,512]{2,1,0:T(8,128)}, u32[]{:S(2)}) copy-start(f32[4,512,512]{2,1,0:T(8,128)} %spectra_ref.1) | copy-start | bytes 12582916
  27.2 3.1 %collective-permute-start = (f32[32,384]{1,0:T(8,128)S(1)}, f32[32,384]{1,0:T(8,128)S(1)}, u32[]{:S(2)}, u32[]{:S(2)}) collective-permute-start(f32[32,384]{1,0:T(8,128)S(1)} %get-tuple-element.11), channel_id=1, source_target_pairs={{0,1},{1,0},{2,3},{3,2},{4,5},{5,4},{6,7},{7,6},{8,9},{9,8},{10,11... | collective-permute-start | bytes 147464 | tf_op jit(solution)/shard_map/ppermute | solution.py:148
  30.3 4.3 %collective-permute-start.3 = (f32[32,384]{1,0:T(8,128)S(1)}, f32[32,384]{1,0:T(8,128)S(1)}, u32[]{:S(2)}, u32[]{:S(2)}) collective-permute-start(f32[32,384]{1,0:T(8,128)S(1)} %select_add_fusion), channel_id=1, source_target_pairs={{0,6},{2,0},{4,2},{6,4},{1,7},{3,1},{5,3},{7,5},{8,14},{10,8},{12,... | collective-permute-start | bytes 147464 | tf_op jit(solution)/shard_map/ppermute | solution.py:148
  32.9 4.4 %collective-permute-start.2 = (f32[32,384]{1,0:T(8,128)S(1)}, f32[32,384]{1,0:T(8,128)S(1)}, u32[]{:S(2)}, u32[]{:S(2)}) collective-permute-start(f32[32,384]{1,0:T(8,128)S(1)} %select_add_fusion), channel_id=1, source_target_pairs={{0,2},{2,4},{4,6},{6,0},{1,3},{3,5},{5,7},{7,1},{8,10},{10,12},{12... | collective-permute-start | bytes 147464 | tf_op jit(solution)/shard_map/ppermute | solution.py:148
  32.9 4.8 %collective-permute-start.1 = (f32[32,384]{1,0:T(8,128)S(1)}, f32[32,384]{1,0:T(8,128)S(1)}, u32[]{:S(2)}, u32[]{:S(2)}) collective-permute-start(f32[32,384]{1,0:T(8,128)S(1)} %select_add_fusion), channel_id=1, source_target_pairs={{0,4},{2,6},{4,0},{6,2},{1,5},{3,7},{5,1},{7,3},{8,12},{10,14},{12... | collective-permute-start | bytes 147464 | tf_op jit(solution)/shard_map/ppermute | solution.py:148
  37.7 2.7 %collective-permute-start.4 = (f32[32,256]{1,0:T(8,128)S(1)}, f32[32,256]{1,0:T(8,128)S(1)}, u32[]{:S(2)}, u32[]{:S(2)}) collective-permute-start(f32[32,256]{1,0:T(8,128)S(1)} %slice.4), channel_id=1, source_target_pairs={{0,1},{1,0},{2,3},{3,2},{4,5},{5,4},{6,7},{7,6},{8,9},{9,8},{10,11... | collective-permute-start | bytes 98312 | tf_op jit(solution)/shard_map/ppermute | solution.py:148

commit v2 on v0

v2 whole, which is shorter than its diff:
```python
import jax
import jax.numpy as jnp
from jax import lax
from jax.experimental import pallas as pl
from jax.experimental.pallas import tpu as pltpu
from jax.sharding import PartitionSpec as P

MZ = 16384
RANK = 32
BINS = 512
HIGHEST = lax.Precision.HIGHEST
F32 = jnp.float32
BF16 = jnp.bfloat16
VMEM = pl.BlockSpec(memory_space=pltpu.VMEM)


def iota(shape, dim):
    return lax.broadcasted_iota(jnp.int32, shape, dim)


def split(x):
    high = x.astype(BF16)
    return high, (x - high.astype(F32)).astype(BF16)


def dot(a, b):
    return jnp.dot(a, b, precision=HIGHEST, preferred_element_type=F32)


def nt_dot(a, b):
    return lax.dot_general(
        a, b, (((1,), (1,)), ((), ())), precision=HIGHEST, preferred_element_type=F32
    )


def as_column(row):
    n = row.shape[1]
    return jnp.sum(jnp.where(iota((n, n), 0) == iota((n, n), 1), row, 0.0), axis=1, keepdims=True)


def contract_kernel(spectra_ref, gathered_ref, out_ref):
    scan = jnp.concatenate([gathered_ref[:, u, :] for u in range(4)], axis=1)
    scan_high, scan_low = split(scan)
    stacked = jnp.concatenate([scan_high, scan_low], axis=0)
    last = gathered_ref.shape[0] - 1
    swapped = lax.axis_index("mz") == last
    total = jnp.zeros((RANK, BINS), F32)
    gram = jnp.zeros((RANK, RANK), F32)
    for s in range(spectra_ref.shape[0]):
        one, two = (gathered_ref[d, 4 + s : 5 + s, :RANK] for d in (0, last))
        one_column, two_column = as_column(one), as_column(two)
        gram = gram + (one_column * one + two_column * two)
        high, low = split(spectra_ref[s])
        both = jnp.dot(stacked, high, preferred_element_type=F32)
        part = both[:RANK] + both[RANK:] + jnp.dot(scan_high, low, preferred_element_type=F32)
        total = total + jnp.where(swapped, one_column, two_column) * part
    out_ref[:, :BINS] = total
    out_ref[:, BINS:] = jnp.zeros((RANK, 128), F32)
    out_ref[:, BINS : BINS + RANK] = gram * nt_dot(scan, scan)


def invert_kernel(total_ref, out_ref):
    system = total_ref[:, BINS : BINS + RANK]
    tiles = RANK // 8
    columns = [
        [jnp.broadcast_to(system[8 * t : 8 * t + 8, j : j + 1], (8, 128)) for t in range(tiles)]
        for j in range(RANK)
    ]
    row, lane = iota((8, 128), 0), iota((8, 128), 1)
    work = [jnp.where(row + 8 * t == lane, 1.0, 0.0) for t in range(tiles)]
    pivots = [jnp.ones((8, 128), F32)] * tiles
    for k in range(RANK):
        top, r = divmod(k, 8)
        pivot = columns[k][top][r : r + 1]
        pivots[top] = jnp.where(row == r, pivot, pivots[top])
        scale = 1.0 / pivot
        factor = [columns[k][t] * scale if t >= top else None for t in range(tiles)]
        factor[top] = jnp.where(row > r, factor[top], 0.0)
        pivot_row = work[top][r : r + 1]
        for t in range(top, tiles):
            work[t] = work[t] - factor[t] * pivot_row
            for j in range(k + 1, min(8 * t + 8, RANK)):
                other = columns[k][j // 8][j % 8 : j % 8 + 1]
                columns[j][t] = columns[j][t] - factor[t] * other
    for t in range(tiles):
        out_ref[8 * t : 8 * t + 8] = (work[t] * lax.rsqrt(pivots[t]))[:, :RANK]


def packed_index(count):
    place = iota((RANK, count), 1)
    whole = place < 512
    row = jnp.where(whole, place >> 5, 16 + ((place - 512) >> 4))
    column = jnp.where(whole, place & 31, 16 + (place & 15))
    return row, column


def solve_kernel(mine_ref, other_ref, factor_ref, raw_ref, packet_ref):
    product = mine_ref[:, :BINS] + other_ref[:, :BINS]
    factor = factor_ref[...]
    raw = dot(factor.T, dot(factor, product))
    slot, core = lax.axis_index("rt"), lax.axis_index("samp")
    tiles = [raw[:, t * 128 : (t + 1) * 128] for t in range(4)]
    own = jnp.where(
        slot < 2,
        jnp.where(slot == 0, tiles[0], tiles[1]),
        jnp.where(slot == 2, tiles[2], tiles[3]),
    )
    raw_ref[...] = jnp.where(core == 0, own, pltpu.roll(own, 64, 1))[:, :64]
    peak = jnp.max(jnp.abs(raw), axis=1, keepdims=True) + 1e-06
    scaled = raw * (1.0 / peak)
    gram = nt_dot(scaled, scaled)
    row, column = packed_index(768)
    spread = jnp.where(iota((RANK, 768), 0) == column, 1.0, 0.0)
    flat = dot(gram, spread)
    flat = jnp.sum(jnp.where(iota((RANK, 768), 0) == row, flat, 0.0), axis=0, keepdims=True)
    lane = iota((RANK, 128), 1)
    peak_row = jnp.sum(
        jnp.where(lane == iota((RANK, 128), 0), peak, 0.0), axis=0, keepdims=True
    )
    packet = jnp.concatenate(
        [flat[:, u * 128 : (u + 1) * 128] for u in range(6)] + [peak_row, jnp.zeros((1, 128), F32)],
        axis=0,
    )
    for d in range(packet_ref.shape[0]):
        packet_ref[d] = packet


def finish_kernel(packets_ref, raw_ref, factor_ref, peak_ref, gram_ref):
    peaks = packets_ref[:, 6, :RANK]
    peak_row = jnp.max(peaks, axis=0, keepdims=True)
    ratio = peaks / peak_row
    row, column = packed_index(768)
    component = iota((RANK, 768), 0)
    of_row, of_column = component == row, component == column
    row_scale = dot(ratio, jnp.where(of_row, 1.0, 0.0))
    column_scale = dot(ratio, jnp.where(of_column, 1.0, 0.0))
    packed = jnp.concatenate([packets_ref[:, u, :] for u in range(6)], axis=1)
    flat = jnp.sum(packed * row_scale * column_scale, axis=0, keepdims=True) * (1.0 / MZ)
    gram = nt_dot(jnp.where(of_row, flat, 0.0), jnp.where(of_column, 1.0, 0.0))
    place = iota((RANK, 768), 1)
    corner = (place < 512) & (column >= 16)
    gram = gram + nt_dot(
        jnp.where(of_column & corner, flat, 0.0), jnp.where(of_row & corner, 1.0, 0.0)
    )
    peak_ref[...] = peak_row
    factor_ref[...] = raw_ref[...] / as_column(peak_row)
    gram_ref[...] = gram


def call(kernel, shapes, ins, name=None):
    return pl.pallas_call(
        kernel,
        out_shape=[jax.ShapeDtypeStruct(s, F32) for s in shapes],
        in_specs=ins,
        out_specs=[VMEM] * len(shapes),
        compiler_params=pltpu.CompilerParams(vmem_limit_bytes=24 * 1024 * 1024),
        name=name,
    )


def shift(x, axis, size, by):
    return lax.ppermute(x, axis, [(i, (i + by) % size) for i in range(size)])


def mixed_groups(chips, slots):
    return [
        [
            (chip * slots + slot) * 2 + (core if chip < chips - 1 else 1 - core)
            for chip in range(chips)
        ]
        for slot in range(slots)
        for core in range(2)
    ]


def local(spectra, sample_factor, scan_factor):
    spectra_other = shift(spectra, "samp", 2, 1)
    sample = jnp.pad(sample_factor.T, ((0, 0), (0, 128 - RANK)))
    packet = jnp.concatenate([scan_factor.reshape(4, 128), sample], axis=0)
    gathered = lax.all_to_all(
        jnp.broadcast_to(packet[None], (RANK,) + packet.shape),
        ("mz", "rt", "samp"),
        0,
        0,
        axis_index_groups=mixed_groups(RANK, 4),
    )
    (partial,) = call(contract_kernel, [(RANK, BINS + 128)], [VMEM] * 2, name="contract")(
        spectra_other, gathered
    )
    far = [shift(partial, "rt", 4, by) for by in (1, 3, 2)]
    mine = (partial + far[2]) + (far[0] + far[1])
    other = shift(mine, "samp", 2, 1)
    (factor,) = call(invert_kernel, [(RANK, RANK)], [VMEM], name="invert")(mine)
    raw, packets = call(solve_kernel, [(RANK, 64), (RANK, 8, 128)], [VMEM] * 3, name="solve")(
        mine, other, factor
    )
    packets = lax.all_to_all(packets, "mz", 0, 0)
    factor, peak, gram = call(
        finish_kernel, [(RANK, 64), (1, RANK), (RANK, RANK)], [VMEM] * 2, name="finish"
    )(packets, raw)
    return (factor, peak.reshape(RANK), gram)


def solution(mesh):
    return jax.shard_map(
        local,
        mesh=mesh,
        in_specs=(P("samp", "rt", "mz"), P(None, "samp"), P("mz", "rt")),
        out_specs=(P(None, ("mz", "rt", "samp")), P(), P()),
        check_vma=False,
    )
```

time: 261 us -> 51.9 us (0.20)
  blocking collectives: 220 us -> 31.7 us
  between operations: 14.1 us -> 0.66 us
  matrix products: 11.3 us -> 0 us
  starting transfers between devices: 0.04 us -> 10.5 us
  other arithmetic: 7.48 us -> 0.73 us
  Pallas kernels: 0 us -> 3.51 us
    psum x2 -> x0, blocking collectives: 86.7 us -> none  [the longest x1 73.6 us: local(): lax.psum(jnp.dot(mz_factor, mz_factor.T, precision=highest), ('mz', 'rt',...]
    pmax x1 -> x0, blocking collectives: 78.4 us -> none  [local(): peak_values = lax.pmax(local_peaks, ('mz', 'rt', 'samp')) + 1e-06]
    all_gather x2 -> x0, blocking collectives: 55.1 us -> none  [the longest x1 40.5 us: local(): scan_block = lax.all_gather(scan_factor, 'mz', axis=0, tiled=True)]
    all_to_all x0 -> x2, blocking collectives: none -> 31.7 us  [the longest x1 19.2 us: local(): lax.all_to_all(jnp.broadcast_to(packet[None], (RANK,) + packet.shape), ('...]
    ppermute x0 -> x5, starting transfers between devices: none -> 10.5 us  [shift(): return lax.ppermute(x, axis, [(i, (i + by) % size) for i in range(size)])]
    dot_general x4 -> x0, matrix products: 10.1 us -> none  [the longest x1 9.57 us: local(): jnp.dot(khatri, spectra.reshape(sample_count * scan_count, spectra.shape[...]
    another operation x5 -> x0, other arithmetic: 6.68 us -> none  [the longest x3 3.6 us: local(): chol_lower = jnp.linalg.cholesky(system)]
    unnamed x2 -> x0, waiting for transfers between devices: 6.15 us -> none
  transfers between devices with their start and end apart: 1 -> 5, of which waited for: 1 -> 2; matrix products, arithmetic and copies ran while one was open for 3% -> 1% of each run, Pallas kernels for 0% -> 1%
where the time goes in v2:
time: 51.9 us; the launch traced here: 51.2 us
  blocking collectives  31.7 us (61%)
  starting transfers between devices  10.5 us (20%)
  waiting for transfers between devices  4.09 us (8%)
  Pallas kernels  3.51 us (7%)
  other arithmetic  0.73 us (1%)
  between operations  0.66 us (1%)
    all_to_all x1, blocking collectives, local(): lax.all_to_all(jnp.broadcast_to(packet[None], (RANK,) + packet.shape), ('...  19.2 us
    all_to_all x1, blocking collectives, local(): packets = lax.all_to_all(packets, 'mz', 0, 0)  12.4 us
    ppermute x5, starting transfers between devices, shift(): return lax.ppermute(x, axis, [(i, (i + by) % size) for i in range(size)])  10.5 us
    ppermute x5, waiting for transfers between devices, shift(): return lax.ppermute(x, axis, [(i, (i + by) % size) for i in range(size)])  4.09 us
    pallas_call x1, Pallas kernels, local(): call(finish_kernel, [(RANK, 64), (1, RANK), (RANK, RANK)], [VMEM] * 2, na...  1.21 us
  transfers between devices with their start and end apart: 5, of which 2 were waited for; matrix products, arithmetic and copies ran while one was open for 1% of the time, Pallas kernels for 1%

profile of v2, /device:TPU:1, one launch (start us, length us, event | category | flops | bytes accessed | tf_op | source)
XLA Modules:
  0.0 51.2 jit_solution(7487947817605645382)
XLA Ops:
  0.6 3.3 %collective-permute-start = (f32[4,512,512]{2,1,0:T(8,128)}, f32[4,512,512]{2,1,0:T(8,128)S(1)}, u32[]{:S(2)}, u32[]{:S(2)}) collective-permute-start(f32[4,512,512]{2,1,0:T(8,128)} %param.3), channel_id=1, source_target_pairs={{0,1},{1,0},{2,3},{3,2},{4,5},{5,4},{6,7},{7,6},{8,9},{9,8},{10,11... | collective-permute-start | bytes 12582920 | tf_op jit(solution)/shard_map/ppermute | solution.py:162
  4.0 0.7 %select_maximum_fusion = f32[8,128]{1,0:T(8,128)S(1)} fusion(f32[4,32]{1,0:T(4,128)} %bitcast.3, f32[4,128]{1,0:T(4,128)} %bitcast.4), kind=kLoop, calls=%fused_computation.1 | loop fusion | flops 3072 | bytes 6656 | tf_op jit(solution)/shard_map/concatenate | solution.py:179
  4.7 19.2 %all_to_all.10.gathered_ref = f32[32,8,128]{2,1,0:T(8,128)S(1)} all-to-all(f32[32,8,128]{2,1,0:T(8,128)S(1)} %broadcast_in_dim.2), channel_id=1, replica_groups={{0,8,16,24,32,40,48,56,64,72,80,88,96,104,112,120,128,136,144,152,160,1..., dimensions={0} | all-to-all | bytes 262144 | tf_op jit(solution)/shard_map/all_to_all | solution.py:180
  23.9 0.0 collective-permute-done.spectra_ref
  23.9 0.9 %contract.1 = f32[32,640]{1,0:T(8,128)S(1)} custom-call(f32[4,512,512]{2,1,0:T(8,128)S(1)} %collective-permute-done.spectra_ref, f32[32,8,128]{2,1,0:T(8,128)S(1)} %all_to_all.10.gathered_ref), custom_call_target="tpu_custom_call" | custom-call | tf_op jit(solution)/shard_map/contract/pallas_call | solution.py:187
  24.8 2.6 %collective-permute-start.3 = (f32[32,640]{1,0:T(8,128)S(1)}, f32[32,640]{1,0:T(8,128)S(1)}, u32[]{:S(2)}, u32[]{:S(2)}) collective-permute-start(f32[32,640]{1,0:T(8,128)S(1)} %contract.1), channel_id=1, source_target_pairs={{0,6},{2,0},{4,2},{6,4},{1,7},{3,1},{5,3},{7,5},{8,14},{10,8},{12,... | collective-permute-start | bytes 245768 | tf_op jit(solution)/shard_map/ppermute | solution.py:162
  27.4 0.0 collective-permute-start.2
  27.4 1.7 %collective-permute-start.1 = (f32[32,640]{1,0:T(8,128)S(1)}, f32[32,640]{1,0:T(8,128)S(1)}, u32[]{:S(2)}, u32[]{:S(2)}) collective-permute-start(f32[32,640]{1,0:T(8,128)S(1)} %contract.1), channel_id=1, source_target_pairs={{0,4},{2,6},{4,0},{6,2},{1,5},{3,7},{5,1},{7,3},{8,12},{10,14},{12... | collective-permute-start | bytes 245768 | tf_op jit(solution)/shard_map/ppermute | solution.py:162
  29.1 0.0 collective-permute-done.3
  29.1 3.6 %collective-permute-done.2 = f32[32,640]{1,0:T(8,128)S(1)} collective-permute-done((f32[32,640]{1,0:T(8,128)S(1)}, f32[32,640]{1,0:T(8,128)S(1)}, u32[]{:S(2)}, u32[]{:S(2)}) %collective-permute-start.2) | collective-permute-done | bytes 81952 | tf_op jit(solution)/shard_map/ppermute | solution.py:162
  32.7 0.0 collective-permute-done.1
  32.8 2.9 %collective-permute-start.4 = (f32[32,640]{1,0:T(8,128)S(1)}, f32[32,640]{1,0:T(8,128)S(1)}, u32[]{:S(2)}, u32[]{:S(2)}) collective-permute-start(f32[32,640]{1,0:T(8,128)S(1)} %add_add_fusion.total_ref.mine_ref), channel_id=1, source_target_pairs={{0,1},{1,0},{2,3},{3,2},{4,5},{5,4},{6,7},{7,6},{8,9},{9,8},{10,11... | collective-permute-start | bytes 245768 | tf_op jit(solution)/shard_map/ppermute | solution.py:162
  35.7 0.5 invert.1.factor_ref
  36.2 0.4 collective-permute-done.4.other_ref
  36.6 0.9 %solve.1 = (f32[32,64]{1,0:T(8,128)S(1)}, f32[32,8,128]{2,1,0:T(8,128)S(1)}) custom-call(f32[32,640]{1,0:T(8,128)S(1)} %add_add_fusion.total_ref.mine_ref, f32[32,640]{1,0:T(8,128)S(1)} %collective-permute-done.4.other_ref, f32[32,32]{1,0:T(8,128)S(1)} %invert.1.factor_ref), custom_call_target="tpu_custom_call" | custom-call | tf_op jit(solution)/shard_map/solve/pallas_call | solution.py:194
  37.5 12.4 %all_to_all.11.packets_ref = f32[32,8,128]{2,1,0:T(8,128)S(1)} all-to-all(f32[32,8,128]{2,1,0:T(8,128)S(1)} %get-tuple-element.8), channel_id=1, replica_groups=mesh['mz'=32,'rt'=4,'samp'=2] {'mz'}, dimensions={0} | all-to-all | bytes 262144 | tf_op jit(solution)/shard_map/all_to_all | solution.py:197
  50.0 1.2 %finish.1 = (f32[32,64]{1,0:T(8,128)}, f32[1,32]{1,0:T(1,128)}, f32[32,32]{1,0:T(8,128)}) custom-call(f32[32,8,128]{2,1,0:T(8,128)S(1)} %all_to_all.11.packets_ref, f32[32,64]{1,0:T(8,128)S(1)} %get-tuple-element.9.raw_ref), custom_call_target="tpu_custom_call" | custom-call | tf_op jit(solution)/shard_map/finish/pallas_call | solution.py:198
  (2 shorter events, 0.0 us)
Async XLA Ops:
  0.6 23.3 %collective-permute-start = (f32[4,512,512]{2,1,0:T(8,128)}, f32[4,512,512]{2,1,0:T(8,128)S(1)}, u32[]{:S(2)}, u32[]{:S(2)}) collective-permute-start(f32[4,512,512]{2,1,0:T(8,128)} %param.3), channel_id=1, source_target_pairs={{0,1},{1,0},{2,3},{3,2},{4,5},{5,4},{6,7},{7,6},{8,9},{9,8},{10,11... | collective-permute-start | bytes 12582920 | tf_op jit(solution)/shard_map/ppermute | solution.py:162
  24.8 4.3 %collective-permute-start.3 = (f32[32,640]{1,0:T(8,128)S(1)}, f32[32,640]{1,0:T(8,128)S(1)}, u32[]{:S(2)}, u32[]{:S(2)}) collective-permute-start(f32[32,640]{1,0:T(8,128)S(1)} %contract.1), channel_id=1, source_target_pairs={{0,6},{2,0},{4,2},{6,4},{1,7},{3,1},{5,3},{7,5},{8,14},{10,8},{12,... | collective-permute-start | bytes 245768 | tf_op jit(solution)/shard_map/ppermute | solution.py:162
  27.4 5.4 %collective-permute-start.2 = (f32[32,640]{1,0:T(8,128)S(1)}, f32[32,640]{1,0:T(8,128)S(1)}, u32[]{:S(2)}, u32[]{:S(2)}) collective-permute-start(f32[32,640]{1,0:T(8,128)S(1)} %contract.1), channel_id=1, source_target_pairs={{0,2},{2,4},{4,6},{6,0},{1,3},{3,5},{5,7},{7,1},{8,10},{10,12},{12... | collective-permute-start | bytes 245768 | tf_op jit(solution)/shard_map/ppermute | solution.py:162
  27.4 5.4 %collective-permute-start.1 = (f32[32,640]{1,0:T(8,128)S(1)}, f32[32,640]{1,0:T(8,128)S(1)}, u32[]{:S(2)}, u32[]{:S(2)}) collective-permute-start(f32[32,640]{1,0:T(8,128)S(1)} %contract.1), channel_id=1, source_target_pairs={{0,4},{2,6},{4,0},{6,2},{1,5},{3,7},{5,1},{7,3},{8,12},{10,14},{12... | collective-permute-start | bytes 245768 | tf_op jit(solution)/shard_map/ppermute | solution.py:162
  32.8 3.8 %collective-permute-start.4 = (f32[32,640]{1,0:T(8,128)S(1)}, f32[32,640]{1,0:T(8,128)S(1)}, u32[]{:S(2)}, u32[]{:S(2)}) collective-permute-start(f32[32,640]{1,0:T(8,128)S(1)} %add_add_fusion.total_ref.mine_ref), channel_id=1, source_target_pairs={{0,1},{1,0},{2,3},{3,2},{4,5},{5,4},{6,7},{7,6},{8,9},{9,8},{10,11... | collective-permute-start | bytes 245768 | tf_op jit(solution)/shard_map/ppermute | solution.py:162

commit v3 on v2

v3 whole, which is shorter than its diff:
```python
import jax
import jax.numpy as jnp
from jax import lax
from jax.experimental import pallas as pl
from jax.experimental.pallas import tpu as pltpu
from jax.sharding import PartitionSpec as P

MZ = 16384
RANK = 32
BINS = 512
FIRST = 18
HIGHEST = lax.Precision.HIGHEST
F32 = jnp.float32
BF16 = jnp.bfloat16
VMEM = pl.BlockSpec(memory_space=pltpu.VMEM)


def iota(shape, dim):
    return lax.broadcasted_iota(jnp.int32, shape, dim)


def split(x):
    high = x.astype(BF16)
    return high, (x - high.astype(F32)).astype(BF16)


def dot(a, b):
    return jnp.dot(a, b, precision=HIGHEST, preferred_element_type=F32)


def nt_dot(a, b, precision=HIGHEST):
    return lax.dot_general(
        a, b, (((1,), (1,)), ((), ())), precision=precision, preferred_element_type=F32
    )


def as_column(row):
    n = row.shape[1]
    return jnp.sum(jnp.where(iota((n, n), 0) == iota((n, n), 1), row, 0.0), axis=1, keepdims=True)


def dist(a, b):
    z, y = abs(a // 4 - b // 4), abs(a % 4 - b % 4)
    return min(z, 8 - z) + min(y, 4 - y)


def ordered(key):
    return [FIRST] + sorted([c for c in range(RANK) if c != FIRST], key=key)


ORDER_A = [(FIRST + i) % RANK for i in range(RANK)]
ORDER_C = ordered(lambda chip: dist(chip, 0))


def in_order(x):
    place = [ORDER_A.index(chip) for chip in range(RANK)]
    pieces, start = [], 0
    for i in range(1, RANK + 1):
        if i == RANK or place[i] != place[i - 1] + 1:
            pieces.append(x[place[start] : place[start] + i - start])
            start = i
    return jnp.concatenate(pieces, axis=0) if len(pieces) > 1 else x


def contract_kernel(spectra_ref, gathered_ref, out_ref):
    scan = jnp.concatenate([gathered_ref[:, u, :] for u in range(4)], axis=1)
    scan = in_order(scan)
    scan_high, scan_low = split(scan)
    stacked = jnp.concatenate([scan_high, scan_low], axis=0)
    last = gathered_ref.shape[0] - 1
    swapped = lax.axis_index("mz") == ORDER_A[-1]
    total = jnp.zeros((RANK, BINS), F32)
    gram = jnp.zeros((RANK, RANK), F32)
    for s in range(spectra_ref.shape[0]):
        one, two = (gathered_ref[d, 4 + s : 5 + s, :RANK] for d in (0, last))
        one_column, two_column = as_column(one), as_column(two)
        gram = gram + (one_column * one + two_column * two)
        high, low = split(spectra_ref[s])
        both = jnp.dot(stacked, high, preferred_element_type=F32)
        part = both[:RANK] + both[RANK:] + jnp.dot(scan_high, low, preferred_element_type=F32)
        total = total + jnp.where(swapped, one_column, two_column) * part
    out_ref[:, :BINS] = total
    out_ref[:, BINS:] = jnp.zeros((RANK, 128), F32)
    out_ref[:, BINS : BINS + RANK] = gram * nt_dot(scan, scan)


def invert_kernel(total_ref, out_ref):
    system = total_ref[:, BINS : BINS + RANK]
    tiles = RANK // 8
    columns = [
        [jnp.broadcast_to(system[8 * t : 8 * t + 8, j : j + 1], (8, 128)) for t in range(tiles)]
        for j in range(RANK)
    ]
    row, lane = iota((8, 128), 0), iota((8, 128), 1)
    work = [jnp.where(row + 8 * t == lane, 1.0, 0.0) for t in range(tiles)]
    pivots = [jnp.ones((8, 128), F32)] * tiles
    for k in range(RANK):
        top, r = divmod(k, 8)
        pivot = columns[k][top][r : r + 1]
        pivots[top] = jnp.where(row == r, pivot, pivots[top])
        scale = 1.0 / pivot
        factor = [columns[k][t] * scale if t >= top else None for t in range(tiles)]
        factor[top] = jnp.where(row > r, factor[top], 0.0)
        pivot_row = work[top][r : r + 1]
        for t in range(top, tiles):
            work[t] = work[t] - factor[t] * pivot_row
            for j in range(k + 1, min(8 * t + 8, RANK)):
                other = columns[k][j // 8][j % 8 : j % 8 + 1]
                columns[j][t] = columns[j][t] - factor[t] * other
    factor = jnp.concatenate(
        [(work[t] * lax.rsqrt(pivots[t]))[:, :RANK] for t in range(tiles)], axis=0
    )
    out_ref[...] = dot(factor.T, factor)


def solve_kernel(mine_ref, other_ref, inverse_ref, raw_ref, packet_ref):
    raw = dot(inverse_ref[...], mine_ref[:, :BINS] + other_ref[:, :BINS])
    slot, core = lax.axis_index("rt"), lax.axis_index("samp")
    tiles = [raw[:, t * 128 : (t + 1) * 128] for t in range(4)]
    own = jnp.where(
        slot < 2,
        jnp.where(slot == 0, tiles[0], tiles[1]),
        jnp.where(slot == 2, tiles[2], tiles[3]),
    )
    raw_ref[...] = jnp.where(core == 0, own, pltpu.roll(own, 64, 1))[:, :64]
    peak = jnp.max(jnp.abs(raw), axis=1, keepdims=True) + 1e-06
    high, low = split(raw * (1.0 / peak))
    both = nt_dot(jnp.concatenate([high, low], axis=0), high, None)
    gram = both[:RANK] + both[RANK:] + nt_dot(high, low, None)
    diagonal = iota((RANK, RANK), 0) == iota((RANK, RANK), 1)
    peak_row = jnp.sum(jnp.where(diagonal, peak, 0.0), axis=0, keepdims=True)
    packet = jnp.concatenate(
        [gram[:8], gram[8:16], gram[16:24, 16:], gram[24:, 16:], jnp.broadcast_to(peak_row, (8, RANK))],
        axis=1,
    )
    for d in range(packet_ref.shape[0]):
        packet_ref[d] = packet


def take_lanes(x, lanes):
    return jnp.take_along_axis(x, lanes, axis=1, mode="promise_in_bounds")


def finish_kernel(packets_ref, raw_ref, factor_ref, peak_ref, gram_ref):
    count = packets_ref.shape[0]
    peaks = packets_ref[0]
    for d in range(1, count):
        peaks = jnp.maximum(peaks, packets_ref[d])
    scale = 1.0 / peaks
    row, lane = iota((8, 128), 0), iota((8, 128), 1)
    block = jnp.where(lane < 64, lane >> 5, jnp.where(lane < 80, 2, 3))
    of_row = 96 + 8 * block + row
    of_column = 96 + jnp.where(lane < 64, lane & 31, 16 + (lane & 15))
    total = jnp.zeros((8, 128), F32)
    for d in range(count):
        packet = packets_ref[d]
        ratio = packet * scale
        total = total + packet * take_lanes(ratio, of_row) * take_lanes(ratio, of_column)
    total = total * (1.0 / MZ)
    peak_ref[...] = peaks[:1, 96:]
    for t in range(RANK // 8):
        rows = slice(8 * t, 8 * t + 8)
        factor_ref[rows] = raw_ref[rows] / take_lanes(peaks, 96 + 8 * t + row)[:, :64]
    upper = jnp.concatenate([total[:, :32], total[:, 32:64]], axis=0)
    corner = jnp.concatenate([total[:, 64:80], total[:, 80:96]], axis=0)
    gram_ref[:16] = upper
    gram_ref[16:] = jnp.concatenate([upper[:, 16:].T, corner], axis=1)


def call(kernel, shapes, ins, name=None):
    return pl.pallas_call(
        kernel,
        out_shape=[jax.ShapeDtypeStruct(s, F32) for s in shapes],
        in_specs=ins,
        out_specs=[VMEM] * len(shapes),
        compiler_params=pltpu.CompilerParams(vmem_limit_bytes=24 * 1024 * 1024),
        name=name,
    )


def shift(x, axis, size, by):
    return lax.ppermute(x, axis, [(i, (i + by) % size) for i in range(size)])


def chip_groups(slots, mixed):
    order = ORDER_A if mixed else ORDER_C
    return [
        [
            (chip * slots + slot) * 2 + (1 - core if mixed and chip == order[-1] else core)
            for chip in order
        ]
        for slot in range(slots)
        for core in range(2)
    ]


def exchange(x, slots, mixed):
    groups = chip_groups(slots, mixed)
    return lax.all_to_all(x, ("mz", "rt", "samp"), 0, 0, axis_index_groups=groups)


def local(spectra, sample_factor, scan_factor):
    spectra_other = shift(spectra, "samp", 2, 1)
    sample = jnp.pad(sample_factor.T, ((0, 0), (0, 128 - RANK)))
    packet = jnp.concatenate([scan_factor.reshape(4, 128), sample], axis=0)
    gathered = exchange(jnp.broadcast_to(packet[None], (RANK,) + packet.shape), 4, True)
    (partial,) = call(contract_kernel, [(RANK, BINS + 128)], [VMEM] * 2, name="contract")(
        spectra_other, gathered
    )
    far = [shift(partial, "rt", 4, by) for by in (1, 3, 2)]
    mine = (partial + far[2]) + (far[0] + far[1])
    other = shift(mine, "samp", 2, 1)
    (inverse,) = call(invert_kernel, [(RANK, RANK)], [VMEM], name="invert")(mine)
    raw, packets = call(solve_kernel, [(RANK, 64), (RANK, 8, 128)], [VMEM] * 3, name="solve")(
        mine, other, inverse
    )
    packets = exchange(packets, 4, False)
    factor, peak, gram = call(
        finish_kernel, [(RANK, 64), (1, RANK), (RANK, RANK)], [VMEM] * 2, name="finish"
    )(packets, raw)
    return (factor, peak.reshape(RANK), gram)


def solution(mesh):
    return jax.shard_map(
        local,
        mesh=mesh,
        in_specs=(P("samp", "rt", "mz"), P(None, "samp"), P("mz", "rt")),
        out_specs=(P(None, ("mz", "rt", "samp")), P(), P()),
        check_vma=False,
    )
```

time: 51.9 us -> 47 us (0.906)
  blocking collectives: 31.7 us -> 28.2 us
  starting transfers between devices: 10.5 us -> 9.83 us
    all_to_all x2, blocking collectives: 31.7 us -> 28.2 us  [exchange(): lax.all_to_all(x, ('mz', 'rt', 'samp'), 0, 0, axis_index_groups=groups)]
    ppermute x5, starting transfers between devices: 10.5 us -> 9.83 us  [shift(): return lax.ppermute(x, axis, [(i, (i + by) % size) for i in range(size)])]
  transfers between devices with their start and end apart: 5 -> 5, of which waited for: 2 -> 2; matrix products, arithmetic and copies ran while one was open for 1% -> 2% of each run, Pallas kernels for 1% -> 2%
where the time goes in v3:
time: 47 us; the launch traced here: 46.8 us
  blocking collectives  28.2 us (60%)
  starting transfers between devices  9.83 us (21%)
  waiting for transfers between devices  4.15 us (9%)
  Pallas kernels  3.15 us (7%)
  other arithmetic  0.73 us (2%)
  between operations  0.66 us (1%)
    all_to_all x2, blocking collectives, exchange(): lax.all_to_all(x, ('mz', 'rt', 'samp'), 0, 0, axis_index_groups=groups)  28.2 us
    ppermute x5, starting transfers between devices, shift(): return lax.ppermute(x, axis, [(i, (i + by) % size) for i in range(size)])  9.83 us
    ppermute x5, waiting for transfers between devices, shift(): return lax.ppermute(x, axis, [(i, (i + by) % size) for i in range(size)])  4.15 us
    pallas_call x1, Pallas kernels, local(): call(finish_kernel, [(RANK, 64), (1, RANK), (RANK, RANK)], [VMEM] * 2, na...  0.99 us
  transfers between devices with their start and end apart: 5, of which 2 were waited for; matrix products, arithmetic and copies ran while one was open for 2% of the time, Pallas kernels for 2%

profile of v3, /device:TPU:1, one launch (start us, length us, event | category | flops | bytes accessed | tf_op | source)
XLA Modules:
  0.0 46.8 jit_solution(5875552065100823311)
XLA Ops:
  0.6 3.3 %collective-permute-start = (f32[4,512,512]{2,1,0:T(8,128)}, f32[4,512,512]{2,1,0:T(8,128)S(1)}, u32[]{:S(2)}, u32[]{:S(2)}) collective-permute-start(f32[4,512,512]{2,1,0:T(8,128)} %param.3), channel_id=1, source_target_pairs={{0,1},{1,0},{2,3},{3,2},{4,5},{5,4},{6,7},{7,6},{8,9},{9,8},{10,11... | collective-permute-start | bytes 12582920 | tf_op jit(solution)/shard_map/ppermute | solution.py:182
  4.0 0.7 %select_maximum_fusion = f32[8,128]{1,0:T(8,128)S(1)} fusion(f32[4,32]{1,0:T(4,128)} %bitcast.3, f32[4,128]{1,0:T(4,128)} %bitcast.4), kind=kLoop, calls=%fused_computation.1 | loop fusion | flops 3072 | bytes 6656 | tf_op jit(solution)/shard_map/concatenate | solution.py:205
  4.7 15.5 %all_to_all.10.gathered_ref = f32[32,8,128]{2,1,0:T(8,128)S(1)} all-to-all(f32[32,8,128]{2,1,0:T(8,128)S(1)} %broadcast_in_dim.2), channel_id=1, replica_groups={{144,152,160,168,176,184,192,200,208,216,224,232,240,248,0,8,16,24,32,4..., dimensions={0} | all-to-all | bytes 262144 | tf_op jit(solution)/shard_map/all_to_all | solution.py:199
  20.2 0.0 collective-permute-done.spectra_ref
  20.2 0.9 %contract.1 = f32[32,640]{1,0:T(8,128)S(1)} custom-call(f32[4,512,512]{2,1,0:T(8,128)S(1)} %collective-permute-done.spectra_ref, f32[32,8,128]{2,1,0:T(8,128)S(1)} %all_to_all.10.gathered_ref), custom_call_target="tpu_custom_call" | custom-call | tf_op jit(solution)/shard_map/contract/pallas_call | solution.py:207
  21.1 2.6 %collective-permute-start.3 = (f32[32,640]{1,0:T(8,128)S(1)}, f32[32,640]{1,0:T(8,128)S(1)}, u32[]{:S(2)}, u32[]{:S(2)}) collective-permute-start(f32[32,640]{1,0:T(8,128)S(1)} %contract.1), channel_id=1, source_target_pairs={{0,6},{2,0},{4,2},{6,4},{1,7},{3,1},{5,3},{7,5},{8,14},{10,8},{12,... | collective-permute-start | bytes 245768 | tf_op jit(solution)/shard_map/ppermute | solution.py:182
  23.6 0.0 collective-permute-start.2
  23.6 1.7 %collective-permute-start.1 = (f32[32,640]{1,0:T(8,128)S(1)}, f32[32,640]{1,0:T(8,128)S(1)}, u32[]{:S(2)}, u32[]{:S(2)}) collective-permute-start(f32[32,640]{1,0:T(8,128)S(1)} %contract.1), channel_id=1, source_target_pairs={{0,4},{2,6},{4,0},{6,2},{1,5},{3,7},{5,1},{7,3},{8,12},{10,14},{12... | collective-permute-start | bytes 245768 | tf_op jit(solution)/shard_map/ppermute | solution.py:182
  25.3 0.0 collective-permute-done.3
  25.4 4.0 %collective-permute-done.2 = f32[32,640]{1,0:T(8,128)S(1)} collective-permute-done((f32[32,640]{1,0:T(8,128)S(1)}, f32[32,640]{1,0:T(8,128)S(1)}, u32[]{:S(2)}, u32[]{:S(2)}) %collective-permute-start.2) | collective-permute-done | bytes 81952 | tf_op jit(solution)/shard_map/ppermute | solution.py:182
  29.3 0.0 collective-permute-done.1
  29.3 2.2 %collective-permute-start.4 = (f32[32,640]{1,0:T(8,128)S(1)}, f32[32,640]{1,0:T(8,128)S(1)}, u32[]{:S(2)}, u32[]{:S(2)}) collective-permute-start(f32[32,640]{1,0:T(8,128)S(1)} %add_add_fusion.total_ref.mine_ref), channel_id=1, source_target_pairs={{0,1},{1,0},{2,3},{3,2},{4,5},{5,4},{6,7},{7,6},{8,9},{9,8},{10,11... | collective-permute-start | bytes 245768 | tf_op jit(solution)/shard_map/ppermute | solution.py:182
  31.6 0.7 %invert.1.inverse_ref = f32[32,32]{1,0:T(8,128)S(1)} custom-call(f32[32,640]{1,0:T(8,128)S(1)} %add_add_fusion.total_ref.mine_ref), custom_call_target="tpu_custom_call" | custom-call | tf_op jit(solution)/shard_map/invert/pallas_call | solution.py:213
  32.3 0.2 collective-permute-done.4.other_ref
  32.5 0.5 %solve.1 = (f32[32,64]{1,0:T(8,128)S(1)}, f32[32,8,128]{2,1,0:T(8,128)S(1)}) custom-call(f32[32,640]{1,0:T(8,128)S(1)} %add_add_fusion.total_ref.mine_ref, f32[32,640]{1,0:T(8,128)S(1)} %collective-permute-done.4.other_ref, f32[32,32]{1,0:T(8,128)S(1)} %invert.1.inverse_ref), custom_call_target="tpu_custom_call" | custom-call | tf_op jit(solution)/shard_map/solve/pallas_call | solution.py:214
  33.0 12.8 %all_to_all.11.packets_ref = f32[32,8,128]{2,1,0:T(8,128)S(1)} all-to-all(f32[32,8,128]{2,1,0:T(8,128)S(1)} %get-tuple-element.8), channel_id=1, replica_groups={{144,0,8,24,32,224,16,40,56,64,192,232,248,48,72,88,96,160,200,216,240,..., dimensions={0} | all-to-all | bytes 262144 | tf_op jit(solution)/shard_map/all_to_all | solution.py:199
  45.8 1.0 %finish.1 = (f32[32,64]{1,0:T(8,128)}, f32[1,32]{1,0:T(1,128)}, f32[32,32]{1,0:T(8,128)}) custom-call(f32[32,8,128]{2,1,0:T(8,128)S(1)} %all_to_all.11.packets_ref, f32[32,64]{1,0:T(8,128)S(1)} %get-tuple-element.9.raw_ref), custom_call_target="tpu_custom_call" | custom-call | tf_op jit(solution)/shard_map/finish/pallas_call | solution.py:218
  (2 shorter events, 0.0 us)
Async XLA Ops:
  0.6 19.5 %collective-permute-start = (f32[4,512,512]{2,1,0:T(8,128)}, f32[4,512,512]{2,1,0:T(8,128)S(1)}, u32[]{:S(2)}, u32[]{:S(2)}) collective-permute-start(f32[4,512,512]{2,1,0:T(8,128)} %param.3), channel_id=1, source_target_pairs={{0,1},{1,0},{2,3},{3,2},{4,5},{5,4},{6,7},{7,6},{8,9},{9,8},{10,11... | collective-permute-start | bytes 12582920 | tf_op jit(solution)/shard_map/ppermute | solution.py:182
  21.1 4.3 %collective-permute-start.3 = (f32[32,640]{1,0:T(8,128)S(1)}, f32[32,640]{1,0:T(8,128)S(1)}, u32[]{:S(2)}, u32[]{:S(2)}) collective-permute-start(f32[32,640]{1,0:T(8,128)S(1)} %contract.1), channel_id=1, source_target_pairs={{0,6},{2,0},{4,2},{6,4},{1,7},{3,1},{5,3},{7,5},{8,14},{10,8},{12,... | collective-permute-start | bytes 245768 | tf_op jit(solution)/shard_map/ppermute | solution.py:182
  23.6 5.7 %collective-permute-start.2 = (f32[32,640]{1,0:T(8,128)S(1)}, f32[32,640]{1,0:T(8,128)S(1)}, u32[]{:S(2)}, u32[]{:S(2)}) collective-permute-start(f32[32,640]{1,0:T(8,128)S(1)} %contract.1), channel_id=1, source_target_pairs={{0,2},{2,4},{4,6},{6,0},{1,3},{3,5},{5,7},{7,1},{8,10},{10,12},{12... | collective-permute-start | bytes 245768 | tf_op jit(solution)/shard_map/ppermute | solution.py:182
  23.6 5.7 %collective-permute-start.1 = (f32[32,640]{1,0:T(8,128)S(1)}, f32[32,640]{1,0:T(8,128)S(1)}, u32[]{:S(2)}, u32[]{:S(2)}) collective-permute-start(f32[32,640]{1,0:T(8,128)S(1)} %contract.1), channel_id=1, source_target_pairs={{0,4},{2,6},{4,0},{6,2},{1,5},{3,7},{5,1},{7,3},{8,12},{10,14},{12... | collective-permute-start | bytes 245768 | tf_op jit(solution)/shard_map/ppermute | solution.py:182
  29.3 3.1 %collective-permute-start.4 = (f32[32,640]{1,0:T(8,128)S(1)}, f32[32,640]{1,0:T(8,128)S(1)}, u32[]{:S(2)}, u32[]{:S(2)}) collective-permute-start(f32[32,640]{1,0:T(8,128)S(1)} %add_add_fusion.total_ref.mine_ref), channel_id=1, source_target_pairs={{0,1},{1,0},{2,3},{3,2},{4,5},{5,4},{6,7},{7,6},{8,9},{9,8},{10,11... | collective-permute-start | bytes 245768 | tf_op jit(solution)/shard_map/ppermute | solution.py:182

commit v4 on v3

--- a/solution.py
+++ b/solution.py
@@ -8,6 +8,7 @@
 MZ = 16384
 RANK = 32
 BINS = 512
+TILES = BINS // 128
 FIRST = 18
 HIGHEST = lax.Precision.HIGHEST
 F32 = jnp.float32
@@ -79,16 +80,20 @@
         both = jnp.dot(stacked, high, preferred_element_type=F32)
         part = both[:RANK] + both[RANK:] + jnp.dot(scan_high, low, preferred_element_type=F32)
         total = total + jnp.where(swapped, one_column, two_column) * part
-    out_ref[:, :BINS] = total
-    out_ref[:, BINS:] = jnp.zeros((RANK, 128), F32)
-    out_ref[:, BINS : BINS + RANK] = gram * nt_dot(scan, scan)
+    for t in range(TILES):
+        out_ref[t * RANK : (t + 1) * RANK] = total[:, t * 128 : (t + 1) * 128]
+    system = gram * nt_dot(scan, scan)
+    out_ref[TILES * RANK :] = jnp.concatenate([system[8 * t : 8 * t + 8] for t in range(4)], axis=1)
 
 
 def invert_kernel(total_ref, out_ref):
-    system = total_ref[:, BINS : BINS + RANK]
+    system = total_ref[TILES * RANK :]
     tiles = RANK // 8
     columns = [
-        [jnp.broadcast_to(system[8 * t : 8 * t + 8, j : j + 1], (8, 128)) for t in range(tiles)]
+        [
+            jnp.broadcast_to(system[:, RANK * t + j : RANK * t + j + 1], (8, 128))
+            for t in range(tiles)
+        ]
         for j in range(RANK)
     ]
     row, lane = iota((8, 128), 0), iota((8, 128), 1)
@@ -114,9 +119,11 @@
 
 
 def solve_kernel(mine_ref, other_ref, inverse_ref, raw_ref, packet_ref):
-    raw = dot(inverse_ref[...], mine_ref[:, :BINS] + other_ref[:, :BINS])
+    parts = [slice(t * RANK, (t + 1) * RANK) for t in range(TILES)]
+    product = jnp.concatenate([mine_ref[part] + other_ref[part] for part in parts], axis=1)
+    raw = dot(inverse_ref[...], product)
     slot, core = lax.axis_index("rt"), lax.axis_index("samp")
-    tiles = [raw[:, t * 128 : (t + 1) * 128] for t in range(4)]
+    tiles = [raw[:, t * 128 : (t + 1) * 128] for t in range(TILES)]
     own = jnp.where(
         slot < 2,
         jnp.where(slot == 0, tiles[0], tiles[1]),
@@ -182,6 +189,11 @@
     return lax.ppermute(x, axis, [(i, (i + by) % size) for i in range(size)])
 
 
+def swap(x, slots, core):
+    pairs = [(i, i ^ (2 * slots + core)) for i in range(8)]
+    return lax.ppermute(x, ("rt", "samp"), pairs)
+
+
 def chip_groups(slots, mixed):
     order = ORDER_A if mixed else ORDER_C
     return [
@@ -204,11 +216,11 @@
     sample = jnp.pad(sample_factor.T, ((0, 0), (0, 128 - RANK)))
     packet = jnp.concatenate([scan_factor.reshape(4, 128), sample], axis=0)
     gathered = exchange(jnp.broadcast_to(packet[None], (RANK,) + packet.shape), 4, True)
-    (partial,) = call(contract_kernel, [(RANK, BINS + 128)], [VMEM] * 2, name="contract")(
+    (partial,) = call(contract_kernel, [(TILES * RANK + 8, 128)], [VMEM] * 2, name="contract")(
         spectra_other, gathered
     )
-    far = [shift(partial, "rt", 4, by) for by in (1, 3, 2)]
-    mine = (partial + far[2]) + (far[0] + far[1])
+    two, three, one = (swap(partial, slots, core) for slots, core in ((2, 1), (3, 0), (1, 1)))
+    mine = (partial + one) + (two + three)
     other = shift(mine, "samp", 2, 1)
     (inverse,) = call(invert_kernel, [(RANK, RANK)], [VMEM], name="invert")(mine)
     raw, packets = call(solve_kernel, [(RANK, 64), (RANK, 8, 128)], [VMEM] * 3, name="solve")(

time: 47 us -> 45.8 us (0.974)
  starting transfers between devices: 9.83 us -> 8.11 us
    ppermute x5 -> x2, starting transfers between devices: 9.83 us -> 4.16 us  [shift(): return lax.ppermute(x, axis, [(i, (i + by) % size) for i in range(size)])]
    ppermute x0 -> x3, waiting for transfers between devices: none -> 4.51 us  [swap(): return lax.ppermute(x, ('rt', 'samp'), pairs)]
    ppermute x5 -> x2, waiting for transfers between devices: 4.15 us -> 0.12 us  [shift(): return lax.ppermute(x, axis, [(i, (i + by) % size) for i in range(size)])]
    ppermute x0 -> x3, starting transfers between devices: none -> 3.95 us  [swap(): return lax.ppermute(x, ('rt', 'samp'), pairs)]
  transfers between devices with their start and end apart: 5 -> 5, of which waited for: 2 -> 3; matrix products, arithmetic and copies ran while one was open for 2% -> 2% of each run, Pallas kernels for 2% -> 2%
where the time goes in v4:
time: 45.8 us; the launch traced here: 45.6 us
  blocking collectives  28.1 us (61%)
  starting transfers between devices  8.11 us (18%)
  waiting for transfers between devices  4.62 us (10%)
  Pallas kernels  3.36 us (7%)
  other arithmetic  0.72 us (2%)
  between operations  0.65 us (1%)
    all_to_all x2, blocking collectives, exchange(): lax.all_to_all(x, ('mz', 'rt', 'samp'), 0, 0, axis_index_groups=groups)  28.1 us
    ppermute x3, waiting for transfers between devices, swap(): return lax.ppermute(x, ('rt', 'samp'), pairs)  4.51 us
    ppermute x2, starting transfers between devices, shift(): return lax.ppermute(x, axis, [(i, (i + by) % size) for i in range(size)])  4.16 us
    ppermute x3, starting transfers between devices, swap(): return lax.ppermute(x, ('rt', 'samp'), pairs)  3.95 us
    pallas_call x1, Pallas kernels, local(): call(contract_kernel, [(TILES * RANK + 8, 128)], [VMEM] * 2, name='contra...  1.04 us
    pallas_call x1, Pallas kernels, local(): call(finish_kernel, [(RANK, 64), (1, RANK), (RANK, RANK)], [VMEM] * 2, na...  0.99 us
  transfers between devices with their start and end apart: 5, of which 3 were waited for; matrix products, arithmetic and copies ran while one was open for 2% of the time, Pallas kernels for 2%

profile of v4, /device:TPU:1, one launch (start us, length us, event | category | flops | bytes accessed | tf_op | source)
XLA Modules:
  0.0 45.6 jit_solution(5141018416280404601)
XLA Ops:
  0.6 3.3 %collective-permute-start = (f32[4,512,512]{2,1,0:T(8,128)}, f32[4,512,512]{2,1,0:T(8,128)S(1)}, u32[]{:S(2)}, u32[]{:S(2)}) collective-permute-start(f32[4,512,512]{2,1,0:T(8,128)} %param.3), channel_id=1, source_target_pairs={{0,1},{1,0},{2,3},{3,2},{4,5},{5,4},{6,7},{7,6},{8,9},{9,8},{10,11... | collective-permute-start | bytes 12582920 | tf_op jit(solution)/shard_map/ppermute | solution.py:189
  4.0 0.7 %select_maximum_fusion = f32[8,128]{1,0:T(8,128)S(1)} fusion(f32[4,32]{1,0:T(4,128)} %bitcast.3, f32[4,128]{1,0:T(4,128)} %bitcast.4), kind=kLoop, calls=%fused_computation.1 | loop fusion | flops 3072 | bytes 6656 | tf_op jit(solution)/shard_map/concatenate | solution.py:217
  4.7 15.5 %all_to_all.10.gathered_ref = f32[32,8,128]{2,1,0:T(8,128)S(1)} all-to-all(f32[32,8,128]{2,1,0:T(8,128)S(1)} %broadcast_in_dim.2), channel_id=1, replica_groups={{144,152,160,168,176,184,192,200,208,216,224,232,240,248,0,8,16,24,32,4..., dimensions={0} | all-to-all | bytes 262144 | tf_op jit(solution)/shard_map/all_to_all | solution.py:211
  20.2 0.0 collective-permute-done.spectra_ref
  20.2 1.0 %contract.1 = f32[136,128]{1,0:T(8,128)S(1)} custom-call(f32[4,512,512]{2,1,0:T(8,128)S(1)} %collective-permute-done.spectra_ref, f32[32,8,128]{2,1,0:T(8,128)S(1)} %all_to_all.10.gathered_ref), custom_call_target="tpu_custom_call" | custom-call | tf_op jit(solution)/shard_map/contract/pallas_call | solution.py:219
  21.2 2.5 %collective-permute-start.3 = (f32[136,128]{1,0:T(8,128)S(1)}, f32[136,128]{1,0:T(8,128)S(1)}, u32[]{:S(2)}, u32[]{:S(2)}) collective-permute-start(f32[136,128]{1,0:T(8,128)S(1)} %contract.1), channel_id=1, source_target_pairs={{0,6},{1,7},{2,4},{3,5},{4,2},{5,3},{6,0},{7,1},{8,14},{9,15},{10,... | collective-permute-start | bytes 208904 | tf_op jit(solution)/shard_map/ppermute | solution.py:194
  23.7 1.4 %collective-permute-start.2 = (f32[136,128]{1,0:T(8,128)S(1)}, f32[136,128]{1,0:T(8,128)S(1)}, u32[]{:S(2)}, u32[]{:S(2)}) collective-permute-start(f32[136,128]{1,0:T(8,128)S(1)} %contract.1), channel_id=1, source_target_pairs={{0,5},{1,4},{2,7},{3,6},{4,1},{5,0},{6,3},{7,2},{8,13},{9,12},{10,... | collective-permute-start | bytes 208904 | tf_op jit(solution)/shard_map/ppermute | solution.py:194
  25.1 0.0 collective-permute-start.1
  25.2 0.5 collective-permute-done.3
  25.6 4.0 %collective-permute-done.2 = f32[136,128]{1,0:T(8,128)S(1)} collective-permute-done((f32[136,128]{1,0:T(8,128)S(1)}, f32[136,128]{1,0:T(8,128)S(1)}, u32[]{:S(2)}, u32[]{:S(2)}) %collective-permute-start.2) | collective-permute-done | bytes 69664 | tf_op jit(solution)/shard_map/ppermute | solution.py:194
  29.7 0.0 collective-permute-done.1
  29.7 0.8 %collective-permute-start.4 = (f32[136,128]{1,0:T(8,128)S(1)}, f32[136,128]{1,0:T(8,128)S(1)}, u32[]{:S(2)}, u32[]{:S(2)}) collective-permute-start(f32[136,128]{1,0:T(8,128)S(1)} %add_add_fusion.total_ref.mine_ref), channel_id=1, source_target_pairs={{0,1},{1,0},{2,3},{3,2},{4,5},{5,4},{6,7},{7,6},{8,9},{9,8},{10,11... | collective-permute-start | bytes 208904 | tf_op jit(solution)/shard_map/ppermute | solution.py:189
  30.5 0.8 %invert.1.inverse_ref = f32[32,32]{1,0:T(8,128)S(1)} custom-call(f32[136,128]{1,0:T(8,128)S(1)} %add_add_fusion.total_ref.mine_ref), custom_call_target="tpu_custom_call" | custom-call | tf_op jit(solution)/shard_map/invert/pallas_call | solution.py:225
  31.3 0.1 collective-permute-done.4.other_ref
  31.4 0.5 %solve.1 = (f32[32,64]{1,0:T(8,128)S(1)}, f32[32,8,128]{2,1,0:T(8,128)S(1)}) custom-call(f32[136,128]{1,0:T(8,128)S(1)} %add_add_fusion.total_ref.mine_ref, f32[136,128]{1,0:T(8,128)S(1)} %collective-permute-done.4.other_ref, f32[32,32]{1,0:T(8,128)S(1)} %invert.1.inverse_ref), custom_call_target="tpu_custom_call" | custom-call | tf_op jit(solution)/shard_map/solve/pallas_call | solution.py:226
  32.0 12.6 %all_to_all.11.packets_ref = f32[32,8,128]{2,1,0:T(8,128)S(1)} all-to-all(f32[32,8,128]{2,1,0:T(8,128)S(1)} %get-tuple-element.8), channel_id=1, replica_groups={{144,0,8,24,32,224,16,40,56,64,192,232,248,48,72,88,96,160,200,216,240,..., dimensions={0} | all-to-all | bytes 262144 | tf_op jit(solution)/shard_map/all_to_all | solution.py:211
  44.6 1.0 %finish.1 = (f32[32,64]{1,0:T(8,128)}, f32[1,32]{1,0:T(1,128)}, f32[32,32]{1,0:T(8,128)}) custom-call(f32[32,8,128]{2,1,0:T(8,128)S(1)} %all_to_all.11.packets_ref, f32[32,64]{1,0:T(8,128)S(1)} %get-tuple-element.9.raw_ref), custom_call_target="tpu_custom_call" | custom-call | tf_op jit(solution)/shard_map/finish/pallas_call | solution.py:230
  (2 shorter events, 0.0 us)
Async XLA Ops:
  0.6 19.5 %collective-permute-start = (f32[4,512,512]{2,1,0:T(8,128)}, f32[4,512,512]{2,1,0:T(8,128)S(1)}, u32[]{:S(2)}, u32[]{:S(2)}) collective-permute-start(f32[4,512,512]{2,1,0:T(8,128)} %param.3), channel_id=1, source_target_pairs={{0,1},{1,0},{2,3},{3,2},{4,5},{5,4},{6,7},{7,6},{8,9},{9,8},{10,11... | collective-permute-start | bytes 12582920 | tf_op jit(solution)/shard_map/ppermute | solution.py:189
  21.2 4.4 %collective-permute-start.3 = (f32[136,128]{1,0:T(8,128)S(1)}, f32[136,128]{1,0:T(8,128)S(1)}, u32[]{:S(2)}, u32[]{:S(2)}) collective-permute-start(f32[136,128]{1,0:T(8,128)S(1)} %contract.1), channel_id=1, source_target_pairs={{0,6},{1,7},{2,4},{3,5},{4,2},{5,3},{6,0},{7,1},{8,14},{9,15},{10,... | collective-permute-start | bytes 208904 | tf_op jit(solution)/shard_map/ppermute | solution.py:194
  23.7 5.9 %collective-permute-start.2 = (f32[136,128]{1,0:T(8,128)S(1)}, f32[136,128]{1,0:T(8,128)S(1)}, u32[]{:S(2)}, u32[]{:S(2)}) collective-permute-start(f32[136,128]{1,0:T(8,128)S(1)} %contract.1), channel_id=1, source_target_pairs={{0,5},{1,4},{2,7},{3,6},{4,1},{5,0},{6,3},{7,2},{8,13},{9,12},{10,... | collective-permute-start | bytes 208904 | tf_op jit(solution)/shard_map/ppermute | solution.py:194
  25.1 4.5 %collective-permute-start.1 = (f32[136,128]{1,0:T(8,128)S(1)}, f32[136,128]{1,0:T(8,128)S(1)}, u32[]{:S(2)}, u32[]{:S(2)}) collective-permute-start(f32[136,128]{1,0:T(8,128)S(1)} %contract.1), channel_id=1, source_target_pairs={{0,3},{1,2},{2,1},{3,0},{4,7},{5,6},{6,5},{7,4},{8,11},{9,10},{10,... | collective-permute-start | bytes 208904 | tf_op jit(solution)/shard_map/ppermute | solution.py:194
  29.7 1.7 %collective-permute-start.4 = (f32[136,128]{1,0:T(8,128)S(1)}, f32[136,128]{1,0:T(8,128)S(1)}, u32[]{:S(2)}, u32[]{:S(2)}) collective-permute-start(f32[136,128]{1,0:T(8,128)S(1)} %add_add_fusion.total_ref.mine_ref), channel_id=1, source_target_pairs={{0,1},{1,0},{2,3},{3,2},{4,5},{5,4},{6,7},{7,6},{8,9},{9,8},{10,11... | collective-permute-start | bytes 208904 | tf_op jit(solution)/shard_map/ppermute | solution.py:189

commit v5 on v4

--- a/solution.py
+++ b/solution.py
@@ -63,8 +63,16 @@
     return jnp.concatenate(pieces, axis=0) if len(pieces) > 1 else x
 
 
+def spread_kernel(packet_ref, out_ref):
+    pieces = [packet_ref[u : u + 1] for u in range(4)]
+    pieces += [packet_ref[4 + s : 5 + s, :RANK] for s in range(4)]
+    row = jnp.concatenate(pieces, axis=1)
+    for d in range(out_ref.shape[0]):
+        out_ref[d] = row
+
+
 def contract_kernel(spectra_ref, gathered_ref, out_ref):
-    scan = jnp.concatenate([gathered_ref[:, u, :] for u in range(4)], axis=1)
+    scan = gathered_ref[:, :BINS]
     scan = in_order(scan)
     scan_high, scan_low = split(scan)
     stacked = jnp.concatenate([scan_high, scan_low], axis=0)
@@ -73,7 +81,7 @@
     total = jnp.zeros((RANK, BINS), F32)
     gram = jnp.zeros((RANK, RANK), F32)
     for s in range(spectra_ref.shape[0]):
-        one, two = (gathered_ref[d, 4 + s : 5 + s, :RANK] for d in (0, last))
+        one, two = (gathered_ref[d : d + 1, BINS + s * RANK : BINS + (s + 1) * RANK] for d in (0, last))
         one_column, two_column = as_column(one), as_column(two)
         gram = gram + (one_column * one + two_column * two)
         high, low = split(spectra_ref[s])
@@ -215,7 +223,9 @@
     spectra_other = shift(spectra, "samp", 2, 1)
     sample = jnp.pad(sample_factor.T, ((0, 0), (0, 128 - RANK)))
     packet = jnp.concatenate([scan_factor.reshape(4, 128), sample], axis=0)
-    gathered = exchange(jnp.broadcast_to(packet[None], (RANK,) + packet.shape), 4, True)
+    width = BINS + 128
+    (packets,) = call(spread_kernel, [(RANK, 1, width)], [VMEM], name="spread")(packet)
+    gathered = exchange(packets, 4, True).reshape(RANK, width)
     (partial,) = call(contract_kernel, [(TILES * RANK + 8, 128)], [VMEM] * 2, name="contract")(
         spectra_other, gathered
     )

time: 45.8 us -> 45.1 us (0.985)
  blocking collectives: 28.1 us -> 27.4 us
    all_to_all x2, blocking collectives: 28.1 us -> 27.4 us  [exchange(): lax.all_to_all(x, ('mz', 'rt', 'samp'), 0, 0, axis_index_groups=groups)]
where the time goes in v5:
time: 45.1 us; the launch traced here: 45 us
  blocking collectives  27.4 us (61%)
  starting transfers between devices  8.28 us (18%)
  waiting for transfers between devices  4.44 us (10%)
  Pallas kernels  3.43 us (8%)
  other arithmetic  0.73 us (2%)
  between operations  0.65 us (1%)
    all_to_all x2, blocking collectives, exchange(): lax.all_to_all(x, ('mz', 'rt', 'samp'), 0, 0, axis_index_groups=groups)  27.4 us
    ppermute x3, waiting for transfers between devices, swap(): return lax.ppermute(x, ('rt', 'samp'), pairs)  4.32 us
    ppermute x2, starting transfers between devices, shift(): return lax.ppermute(x, axis, [(i, (i + by) % size) for i in range(size)])  4.2 us
    ppermute x3, starting transfers between devices, swap(): return lax.ppermute(x, ('rt', 'samp'), pairs)  4.07 us
    pallas_call x1, Pallas kernels, local(): call(contract_kernel, [(TILES * RANK + 8, 128)], [VMEM] * 2, name='contra...  1.03 us
    pallas_call x1, Pallas kernels, local(): call(finish_kernel, [(RANK, 64), (1, RANK), (RANK, RANK)], [VMEM] * 2, na...  0.99 us
  transfers between devices with their start and end apart: 5, of which 3 were waited for; matrix products, arithmetic and copies ran while one was open for 2% of the time, Pallas kernels for 2%

profile of v5, /device:TPU:1, one launch (start us, length us, event | category | flops | bytes accessed | tf_op | source)
XLA Modules:
  0.0 45.0 jit_solution(6459554948364944177)
XLA Ops:
  0.6 3.3 %collective-permute-start = (f32[4,512,512]{2,1,0:T(8,128)}, f32[4,512,512]{2,1,0:T(8,128)S(1)}, u32[]{:S(2)}, u32[]{:S(2)}) collective-permute-start(f32[4,512,512]{2,1,0:T(8,128)} %param.3), channel_id=1, source_target_pairs={{0,1},{1,0},{2,3},{3,2},{4,5},{5,4},{6,7},{7,6},{8,9},{9,8},{10,11... | collective-permute-start | bytes 12582920 | tf_op jit(solution)/shard_map/ppermute | solution.py:197
  4.0 0.7 %select_maximum_fusion.packet_ref = f32[8,128]{1,0:T(8,128)S(1)} fusion(f32[4,32]{1,0:T(4,128)} %bitcast.7, f32[4,128]{1,0:T(4,128)} %bitcast.8), kind=kLoop, calls=%fused_computation.2 | loop fusion | flops 3072 | bytes 6656 | tf_op jit(solution)/shard_map/concatenate | solution.py:225
  4.7 0.1 spread.1
  4.8 14.3 %all_to_all.10 = f32[32,1,640]{2,1,0:T(1,128)S(1)} all-to-all(f32[32,1,640]{2,1,0:T(1,128)S(1)} %spread.1), channel_id=1, replica_groups={{144,152,160,168,176,184,192,200,208,216,224,232,240,248,0,8,16,24,32,4..., dimensions={0} | all-to-all | bytes 163840 | tf_op jit(solution)/shard_map/all_to_all | solution.py:219
  19.0 0.0 collective-permute-done.spectra_ref
  19.0 1.0 %contract.1 = f32[136,128]{1,0:T(8,128)S(1)} custom-call(f32[4,512,512]{2,1,0:T(8,128)S(1)} %collective-permute-done.spectra_ref, f32[32,640]{1,0:T(8,128)S(1)} %bitcast.6), custom_call_target="tpu_custom_call" | custom-call | tf_op jit(solution)/shard_map/contract/pallas_call | solution.py:229
  20.1 2.5 %collective-permute-start.3 = (f32[136,128]{1,0:T(8,128)S(1)}, f32[136,128]{1,0:T(8,128)S(1)}, u32[]{:S(2)}, u32[]{:S(2)}) collective-permute-start(f32[136,128]{1,0:T(8,128)S(1)} %contract.1), channel_id=1, source_target_pairs={{0,6},{1,7},{2,4},{3,5},{4,2},{5,3},{6,0},{7,1},{8,14},{9,15},{10,... | collective-permute-start | bytes 208904 | tf_op jit(solution)/shard_map/ppermute | solution.py:202
  22.6 1.6 %collective-permute-start.2 = (f32[136,128]{1,0:T(8,128)S(1)}, f32[136,128]{1,0:T(8,128)S(1)}, u32[]{:S(2)}, u32[]{:S(2)}) collective-permute-start(f32[136,128]{1,0:T(8,128)S(1)} %contract.1), channel_id=1, source_target_pairs={{0,5},{1,4},{2,7},{3,6},{4,1},{5,0},{6,3},{7,2},{8,13},{9,12},{10,... | collective-permute-start | bytes 208904 | tf_op jit(solution)/shard_map/ppermute | solution.py:202
  24.1 0.0 collective-permute-start.1
  24.1 0.3 collective-permute-done.3
  24.5 4.0 %collective-permute-done.2 = f32[136,128]{1,0:T(8,128)S(1)} collective-permute-done((f32[136,128]{1,0:T(8,128)S(1)}, f32[136,128]{1,0:T(8,128)S(1)}, u32[]{:S(2)}, u32[]{:S(2)}) %collective-permute-start.2) | collective-permute-done | bytes 69664 | tf_op jit(solution)/shard_map/ppermute | solution.py:202
  28.5 0.0 collective-permute-done.1
  28.5 0.9 %collective-permute-start.4 = (f32[136,128]{1,0:T(8,128)S(1)}, f32[136,128]{1,0:T(8,128)S(1)}, u32[]{:S(2)}, u32[]{:S(2)}) collective-permute-start(f32[136,128]{1,0:T(8,128)S(1)} %add_add_fusion.total_ref.mine_ref), channel_id=1, source_target_pairs={{0,1},{1,0},{2,3},{3,2},{4,5},{5,4},{6,7},{7,6},{8,9},{9,8},{10,11... | collective-permute-start | bytes 208904 | tf_op jit(solution)/shard_map/ppermute | solution.py:197
  29.4 0.8 %invert.1.inverse_ref = f32[32,32]{1,0:T(8,128)S(1)} custom-call(f32[136,128]{1,0:T(8,128)S(1)} %add_add_fusion.total_ref.mine_ref), custom_call_target="tpu_custom_call" | custom-call | tf_op jit(solution)/shard_map/invert/pallas_call | solution.py:235
  30.2 0.1 collective-permute-done.4.other_ref
  30.3 0.5 %solve.1 = (f32[32,64]{1,0:T(8,128)S(1)}, f32[32,8,128]{2,1,0:T(8,128)S(1)}) custom-call(f32[136,128]{1,0:T(8,128)S(1)} %add_add_fusion.total_ref.mine_ref, f32[136,128]{1,0:T(8,128)S(1)} %collective-permute-done.4.other_ref, f32[32,32]{1,0:T(8,128)S(1)} %invert.1.inverse_ref), custom_call_target="tpu_custom_call" | custom-call | tf_op jit(solution)/shard_map/solve/pallas_call | solution.py:236
  30.8 13.2 %all_to_all.11.packets_ref = f32[32,8,128]{2,1,0:T(8,128)S(1)} all-to-all(f32[32,8,128]{2,1,0:T(8,128)S(1)} %get-tuple-element.8), channel_id=1, replica_groups={{144,0,8,24,32,224,16,40,56,64,192,232,248,48,72,88,96,160,200,216,240,..., dimensions={0} | all-to-all | bytes 262144 | tf_op jit(solution)/shard_map/all_to_all | solution.py:219
  44.0 1.0 %finish.1 = (f32[32,64]{1,0:T(8,128)}, f32[1,32]{1,0:T(1,128)}, f32[32,32]{1,0:T(8,128)}) custom-call(f32[32,8,128]{2,1,0:T(8,128)S(1)} %all_to_all.11.packets_ref, f32[32,64]{1,0:T(8,128)S(1)} %get-tuple-element.9.raw_ref), custom_call_target="tpu_custom_call" | custom-call | tf_op jit(solution)/shard_map/finish/pallas_call | solution.py:240
  (2 shorter events, 0.0 us)
Async XLA Ops:
  0.6 18.4 %collective-permute-start = (f32[4,512,512]{2,1,0:T(8,128)}, f32[4,512,512]{2,1,0:T(8,128)S(1)}, u32[]{:S(2)}, u32[]{:S(2)}) collective-permute-start(f32[4,512,512]{2,1,0:T(8,128)} %param.3), channel_id=1, source_target_pairs={{0,1},{1,0},{2,3},{3,2},{4,5},{5,4},{6,7},{7,6},{8,9},{9,8},{10,11... | collective-permute-start | bytes 12582920 | tf_op jit(solution)/shard_map/ppermute | solution.py:197
  20.1 4.4 %collective-permute-start.3 = (f32[136,128]{1,0:T(8,128)S(1)}, f32[136,128]{1,0:T(8,128)S(1)}, u32[]{:S(2)}, u32[]{:S(2)}) collective-permute-start(f32[136,128]{1,0:T(8,128)S(1)} %contract.1), channel_id=1, source_target_pairs={{0,6},{1,7},{2,4},{3,5},{4,2},{5,3},{6,0},{7,1},{8,14},{9,15},{10,... | collective-permute-start | bytes 208904 | tf_op jit(solution)/shard_map/ppermute | solution.py:202
  22.6 5.9 %collective-permute-start.2 = (f32[136,128]{1,0:T(8,128)S(1)}, f32[136,128]{1,0:T(8,128)S(1)}, u32[]{:S(2)}, u32[]{:S(2)}) collective-permute-start(f32[136,128]{1,0:T(8,128)S(1)} %contract.1), channel_id=1, source_target_pairs={{0,5},{1,4},{2,7},{3,6},{4,1},{5,0},{6,3},{7,2},{8,13},{9,12},{10,... | collective-permute-start | bytes 208904 | tf_op jit(solution)/shard_map/ppermute | solution.py:202
  24.1 4.3 %collective-permute-start.1 = (f32[136,128]{1,0:T(8,128)S(1)}, f32[136,128]{1,0:T(8,128)S(1)}, u32[]{:S(2)}, u32[]{:S(2)}) collective-permute-start(f32[136,128]{1,0:T(8,128)S(1)} %contract.1), channel_id=1, source_target_pairs={{0,3},{1,2},{2,1},{3,0},{4,7},{5,6},{6,5},{7,4},{8,11},{9,10},{10,... | collective-permute-start | bytes 208904 | tf_op jit(solution)/shard_map/ppermute | solution.py:202
  28.5 1.8 %collective-permute-start.4 = (f32[136,128]{1,0:T(8,128)S(1)}, f32[136,128]{1,0:T(8,128)S(1)}, u32[]{:S(2)}, u32[]{:S(2)}) collective-permute-start(f32[136,128]{1,0:T(8,128)S(1)} %add_add_fusion.total_ref.mine_ref), channel_id=1, source_target_pairs={{0,1},{1,0},{2,3},{3,2},{4,5},{5,4},{6,7},{7,6},{8,9},{9,8},{10,11... | collective-permute-start | bytes 208904 | tf_op jit(solution)/shard_map/ppermute | solution.py:197

commit v6 on v5

--- a/solution.py
+++ b/solution.py
@@ -144,9 +144,9 @@
     gram = both[:RANK] + both[RANK:] + nt_dot(high, low, None)
     diagonal = iota((RANK, RANK), 0) == iota((RANK, RANK), 1)
     peak_row = jnp.sum(jnp.where(diagonal, peak, 0.0), axis=0, keepdims=True)
+    blocks = jnp.concatenate([gram[8 * t : 8 * t + 8, 8 * t :] for t in range(4)], axis=1)
     packet = jnp.concatenate(
-        [gram[:8], gram[8:16], gram[16:24, 16:], gram[24:, 16:], jnp.broadcast_to(peak_row, (8, RANK))],
-        axis=1,
+        [blocks[u : u + 1] for u in range(8)] + [peak_row, jnp.zeros((1, 96), F32)], axis=1
     )
     for d in range(packet_ref.shape[0]):
         packet_ref[d] = packet
@@ -157,29 +157,39 @@
 
 
 def finish_kernel(packets_ref, raw_ref, factor_ref, peak_ref, gram_ref):
-    count = packets_ref.shape[0]
-    peaks = packets_ref[0]
-    for d in range(1, count):
-        peaks = jnp.maximum(peaks, packets_ref[d])
-    scale = 1.0 / peaks
-    row, lane = iota((8, 128), 0), iota((8, 128), 1)
-    block = jnp.where(lane < 64, lane >> 5, jnp.where(lane < 80, 2, 3))
-    of_row = 96 + 8 * block + row
-    of_column = 96 + jnp.where(lane < 64, lane & 31, 16 + (lane & 15))
-    total = jnp.zeros((8, 128), F32)
-    for d in range(count):
-        packet = packets_ref[d]
-        ratio = packet * scale
-        total = total + packet * take_lanes(ratio, of_row) * take_lanes(ratio, of_column)
-    total = total * (1.0 / MZ)
-    peak_ref[...] = peaks[:1, 96:]
-    for t in range(RANK // 8):
-        rows = slice(8 * t, 8 * t + 8)
-        factor_ref[rows] = raw_ref[rows] / take_lanes(peaks, 96 + 8 * t + row)[:, :64]
-    upper = jnp.concatenate([total[:, :32], total[:, 32:64]], axis=0)
-    corner = jnp.concatenate([total[:, 64:80], total[:, 80:96]], axis=0)
-    gram_ref[:16] = upper
-    gram_ref[16:] = jnp.concatenate([upper[:, 16:].T, corner], axis=1)
+    width = 80
+    last = packets_ref[:, 8 * width :]
+    peak_row = jnp.max(last, axis=0, keepdims=True)
+    ratio = last / peak_row
+    tiles = []
+    for t in range(5):
+        place = iota((8, 128), 1) + 128 * t
+        u, lane = place // width, place % width
+        block = jnp.where(lane < 32, 0, jnp.where(lane < 56, 1, jnp.where(lane < 72, 2, 3)))
+        column = jnp.where(
+            lane < 32, lane, jnp.where(lane < 56, lane - 24, jnp.where(lane < 72, lane - 40, lane - 48))
+        )
+        total = jnp.zeros((8, 128), F32)
+        for d in range(0, packets_ref.shape[0], 8):
+            scale = ratio[d : d + 8]
+            packet = packets_ref[d : d + 8, 128 * t : 128 * t + 128]
+            total = total + packet * take_lanes(scale, 8 * block + u) * take_lanes(scale, column)
+        tiles.append(jnp.sum(total, axis=0, keepdims=True))
+    flat = jnp.concatenate(tiles, axis=1) * (1.0 / MZ)
+    blocks = jnp.concatenate([flat[:, width * u : width * (u + 1)] for u in range(8)], axis=0)
+    upper = jnp.concatenate(
+        [
+            blocks[:, :32],
+            jnp.concatenate([jnp.zeros((8, 8), F32), blocks[:, 32:56]], axis=1),
+            jnp.concatenate([jnp.zeros((8, 16), F32), blocks[:, 56:72]], axis=1),
+            jnp.concatenate([jnp.zeros((8, 24), F32), blocks[:, 72:80]], axis=1),
+        ],
+        axis=0,
+    )
+    row, column = iota((RANK, RANK), 0), iota((RANK, RANK), 1)
+    gram_ref[...] = jnp.where((row >> 3) <= (column >> 3), upper, upper.T)
+    peak_ref[...] = peak_row[:, :RANK]
+    factor_ref[...] = raw_ref[...] / as_column(peak_row[:, :RANK])
 
 
 def call(kernel, shapes, ins, name=None):
@@ -233,10 +243,10 @@
     mine = (partial + one) + (two + three)
     other = shift(mine, "samp", 2, 1)
     (inverse,) = call(invert_kernel, [(RANK, RANK)], [VMEM], name="invert")(mine)
-    raw, packets = call(solve_kernel, [(RANK, 64), (RANK, 8, 128)], [VMEM] * 3, name="solve")(
+    raw, packets = call(solve_kernel, [(RANK, 64), (RANK, 1, 768)], [VMEM] * 3, name="solve")(
         mine, other, inverse
     )
-    packets = exchange(packets, 4, False)
+    packets = exchange(packets, 4, False).reshape(RANK, 768)
     factor, peak, gram = call(
         finish_kernel, [(RANK, 64), (1, RANK), (RANK, RANK)], [VMEM] * 2, name="finish"
     )(packets, raw)

time: 45.1 us -> 44.7 us (level)
  blocking collectives: 27.4 us -> 26.8 us
    all_to_all x2, blocking collectives: 27.4 us -> 26.8 us  [exchange(): lax.all_to_all(x, ('mz', 'rt', 'samp'), 0, 0, axis_index_groups=groups)]
where the time goes in v6:
time: 44.7 us; the launch traced here: 44.5 us
  blocking collectives  26.8 us (60%)
  starting transfers between devices  8.28 us (19%)
  waiting for transfers between devices  4.44 us (10%)
  Pallas kernels  3.52 us (8%)
  other arithmetic  0.72 us (2%)
  between operations  0.66 us (1%)
    all_to_all x2, blocking collectives, exchange(): lax.all_to_all(x, ('mz', 'rt', 'samp'), 0, 0, axis_index_groups=groups)  26.8 us
    ppermute x3, waiting for transfers between devices, swap(): return lax.ppermute(x, ('rt', 'samp'), pairs)  4.32 us
    ppermute x2, starting transfers between devices, shift(): return lax.ppermute(x, axis, [(i, (i + by) % size) for i in range(size)])  4.2 us
    ppermute x3, starting transfers between devices, swap(): return lax.ppermute(x, ('rt', 'samp'), pairs)  4.07 us
    pallas_call x1, Pallas kernels, local(): call(contract_kernel, [(TILES * RANK + 8, 128)], [VMEM] * 2, name='contra...  1.03 us
    pallas_call x1, Pallas kernels, local(): call(finish_kernel, [(RANK, 64), (1, RANK), (RANK, RANK)], [VMEM] * 2, na...  1.01 us
  transfers between devices with their start and end apart: 5, of which 3 were waited for; matrix products, arithmetic and copies ran while one was open for 2% of the time, Pallas kernels for 2%

profile of v6, /device:TPU:1, one launch (start us, length us, event | category | flops | bytes accessed | tf_op | source)
XLA Modules:
  0.0 44.5 jit_solution(825069095310073530)
XLA Ops:
  0.6 3.3 %collective-permute-start = (f32[4,512,512]{2,1,0:T(8,128)}, f32[4,512,512]{2,1,0:T(8,128)S(1)}, u32[]{:S(2)}, u32[]{:S(2)}) collective-permute-start(f32[4,512,512]{2,1,0:T(8,128)} %param.3), channel_id=1, source_target_pairs={{0,1},{1,0},{2,3},{3,2},{4,5},{5,4},{6,7},{7,6},{8,9},{9,8},{10,11... | collective-permute-start | bytes 12582920 | tf_op jit(solution)/shard_map/ppermute | solution.py:207
  4.0 0.7 %select_maximum_fusion.packet_ref = f32[8,128]{1,0:T(8,128)S(1)} fusion(f32[4,32]{1,0:T(4,128)} %bitcast.11, f32[4,128]{1,0:T(4,128)} %bitcast.12), kind=kLoop, calls=%fused_computation.3 | loop fusion | flops 3072 | bytes 6656 | tf_op jit(solution)/shard_map/concatenate | solution.py:235
  4.7 0.1 spread.1
  4.8 14.3 %all_to_all.10 = f32[32,1,640]{2,1,0:T(1,128)S(1)} all-to-all(f32[32,1,640]{2,1,0:T(1,128)S(1)} %spread.1), channel_id=1, replica_groups={{144,152,160,168,176,184,192,200,208,216,224,232,240,248,0,8,16,24,32,4..., dimensions={0} | all-to-all | bytes 163840 | tf_op jit(solution)/shard_map/all_to_all | solution.py:229
  19.0 0.0 collective-permute-done.spectra_ref
  19.0 1.0 %contract.1 = f32[136,128]{1,0:T(8,128)S(1)} custom-call(f32[4,512,512]{2,1,0:T(8,128)S(1)} %collective-permute-done.spectra_ref, f32[32,640]{1,0:T(8,128)S(1)} %bitcast.10), custom_call_target="tpu_custom_call" | custom-call | tf_op jit(solution)/shard_map/contract/pallas_call | solution.py:239
  20.1 2.5 %collective-permute-start.3 = (f32[136,128]{1,0:T(8,128)S(1)}, f32[136,128]{1,0:T(8,128)S(1)}, u32[]{:S(2)}, u32[]{:S(2)}) collective-permute-start(f32[136,128]{1,0:T(8,128)S(1)} %contract.1), channel_id=1, source_target_pairs={{0,6},{1,7},{2,4},{3,5},{4,2},{5,3},{6,0},{7,1},{8,14},{9,15},{10,... | collective-permute-start | bytes 208904 | tf_op jit(solution)/shard_map/ppermute | solution.py:212
  22.6 1.6 %collective-permute-start.2 = (f32[136,128]{1,0:T(8,128)S(1)}, f32[136,128]{1,0:T(8,128)S(1)}, u32[]{:S(2)}, u32[]{:S(2)}) collective-permute-start(f32[136,128]{1,0:T(8,128)S(1)} %contract.1), channel_id=1, source_target_pairs={{0,5},{1,4},{2,7},{3,6},{4,1},{5,0},{6,3},{7,2},{8,13},{9,12},{10,... | collective-permute-start | bytes 208904 | tf_op jit(solution)/shard_map/ppermute | solution.py:212
  24.1 0.0 collective-permute-start.1
  24.1 0.3 collective-permute-done.3
  24.5 4.0 %collective-permute-done.2 = f32[136,128]{1,0:T(8,128)S(1)} collective-permute-done((f32[136,128]{1,0:T(8,128)S(1)}, f32[136,128]{1,0:T(8,128)S(1)}, u32[]{:S(2)}, u32[]{:S(2)}) %collective-permute-start.2) | collective-permute-done | bytes 69664 | tf_op jit(solution)/shard_map/ppermute | solution.py:212
  28.5 0.0 collective-permute-done.1
  28.5 0.9 %collective-permute-start.4 = (f32[136,128]{1,0:T(8,128)S(1)}, f32[136,128]{1,0:T(8,128)S(1)}, u32[]{:S(2)}, u32[]{:S(2)}) collective-permute-start(f32[136,128]{1,0:T(8,128)S(1)} %add_add_fusion.total_ref.mine_ref), channel_id=1, source_target_pairs={{0,1},{1,0},{2,3},{3,2},{4,5},{5,4},{6,7},{7,6},{8,9},{9,8},{10,11... | collective-permute-start | bytes 208904 | tf_op jit(solution)/shard_map/ppermute | solution.py:207
  29.4 0.8 %invert.1.inverse_ref = f32[32,32]{1,0:T(8,128)S(1)} custom-call(f32[136,128]{1,0:T(8,128)S(1)} %add_add_fusion.total_ref.mine_ref), custom_call_target="tpu_custom_call" | custom-call | tf_op jit(solution)/shard_map/invert/pallas_call | solution.py:245
  30.2 0.1 collective-permute-done.4.other_ref
  30.3 0.6 %solve.1 = (f32[32,64]{1,0:T(8,128)S(1)}, f32[32,1,768]{2,1,0:T(1,128)S(1)}) custom-call(f32[136,128]{1,0:T(8,128)S(1)} %add_add_fusion.total_ref.mine_ref, f32[136,128]{1,0:T(8,128)S(1)} %collective-permute-done.4.other_ref, f32[32,32]{1,0:T(8,128)S(1)} %invert.1.inverse_ref), custom_call_target="tpu_custom_call" | custom-call | tf_op jit(solution)/shard_map/solve/pallas_call | solution.py:246
  30.9 12.6 %all_to_all.11 = f32[32,1,768]{2,1,0:T(1,128)S(1)} all-to-all(f32[32,1,768]{2,1,0:T(1,128)S(1)} %get-tuple-element.8), channel_id=1, replica_groups={{144,0,8,24,32,224,16,40,56,64,192,232,248,48,72,88,96,160,200,216,240,..., dimensions={0} | all-to-all | bytes 196608 | tf_op jit(solution)/shard_map/all_to_all | solution.py:229
  43.5 1.0 %finish.1 = (f32[32,64]{1,0:T(8,128)}, f32[1,32]{1,0:T(1,128)}, f32[32,32]{1,0:T(8,128)}) custom-call(f32[32,768]{1,0:T(8,128)S(1)} %bitcast.9, f32[32,64]{1,0:T(8,128)S(1)} %get-tuple-element.9.raw_ref), custom_call_target="tpu_custom_call" | custom-call | tf_op jit(solution)/shard_map/finish/pallas_call | solution.py:250
  (3 shorter events, 0.0 us)
Async XLA Ops:
  0.6 18.4 %collective-permute-start = (f32[4,512,512]{2,1,0:T(8,128)}, f32[4,512,512]{2,1,0:T(8,128)S(1)}, u32[]{:S(2)}, u32[]{:S(2)}) collective-permute-start(f32[4,512,512]{2,1,0:T(8,128)} %param.3), channel_id=1, source_target_pairs={{0,1},{1,0},{2,3},{3,2},{4,5},{5,4},{6,7},{7,6},{8,9},{9,8},{10,11... | collective-permute-start | bytes 12582920 | tf_op jit(solution)/shard_map/ppermute | solution.py:207
  20.1 4.4 %collective-permute-start.3 = (f32[136,128]{1,0:T(8,128)S(1)}, f32[136,128]{1,0:T(8,128)S(1)}, u32[]{:S(2)}, u32[]{:S(2)}) collective-permute-start(f32[136,128]{1,0:T(8,128)S(1)} %contract.1), channel_id=1, source_target_pairs={{0,6},{1,7},{2,4},{3,5},{4,2},{5,3},{6,0},{7,1},{8,14},{9,15},{10,... | collective-permute-start | bytes 208904 | tf_op jit(solution)/shard_map/ppermute | solution.py:212
  22.6 5.9 %collective-permute-start.2 = (f32[136,128]{1,0:T(8,128)S(1)}, f32[136,128]{1,0:T(8,128)S(1)}, u32[]{:S(2)}, u32[]{:S(2)}) collective-permute-start(f32[136,128]{1,0:T(8,128)S(1)} %contract.1), channel_id=1, source_target_pairs={{0,5},{1,4},{2,7},{3,6},{4,1},{5,0},{6,3},{7,2},{8,13},{9,12},{10,... | collective-permute-start | bytes 208904 | tf_op jit(solution)/shard_map/ppermute | solution.py:212
  24.1 4.3 %collective-permute-start.1 = (f32[136,128]{1,0:T(8,128)S(1)}, f32[136,128]{1,0:T(8,128)S(1)}, u32[]{:S(2)}, u32[]{:S(2)}) collective-permute-start(f32[136,128]{1,0:T(8,128)S(1)} %contract.1), channel_id=1, source_target_pairs={{0,3},{1,2},{2,1},{3,0},{4,7},{5,6},{6,5},{7,4},{8,11},{9,10},{10,... | collective-permute-start | bytes 208904 | tf_op jit(solution)/shard_map/ppermute | solution.py:212
  28.5 1.8 %collective-permute-start.4 = (f32[136,128]{1,0:T(8,128)S(1)}, f32[136,128]{1,0:T(8,128)S(1)}, u32[]{:S(2)}, u32[]{:S(2)}) collective-permute-start(f32[136,128]{1,0:T(8,128)S(1)} %add_add_fusion.total_ref.mine_ref), channel_id=1, source_target_pairs={{0,1},{1,0},{2,3},{3,2},{4,5},{5,4},{6,7},{7,6},{8,9},{9,8},{10,11... | collective-permute-start | bytes 208904 | tf_op jit(solution)/shard_map/ppermute | solution.py:207

commit v7 on v6

--- a/solution.py
+++ b/solution.py
@@ -144,10 +144,13 @@
     gram = both[:RANK] + both[RANK:] + nt_dot(high, low, None)
     diagonal = iota((RANK, RANK), 0) == iota((RANK, RANK), 1)
     peak_row = jnp.sum(jnp.where(diagonal, peak, 0.0), axis=0, keepdims=True)
+    row, column = iota((RANK, RANK), 0), iota((RANK, RANK), 1)
+    within = (row >> 3) == (column >> 3)
+    turned = jnp.concatenate([peak_row[:, 7:], peak_row[:, :7]], axis=1)
+    gram = jnp.where(within & ((row & 7) == 7) & ((column & 7) < 7), peak_row, gram)
+    gram = jnp.where(within & ((row & 7) == 6) & ((column & 7) == 0), turned, gram)
     blocks = jnp.concatenate([gram[8 * t : 8 * t + 8, 8 * t :] for t in range(4)], axis=1)
-    packet = jnp.concatenate(
-        [blocks[u : u + 1] for u in range(8)] + [peak_row, jnp.zeros((1, 96), F32)], axis=1
-    )
+    packet = jnp.concatenate([blocks[u : u + 1] for u in range(8)], axis=1)
     for d in range(packet_ref.shape[0]):
         packet_ref[d] = packet
 
@@ -158,9 +161,18 @@
 
 def finish_kernel(packets_ref, raw_ref, factor_ref, peak_ref, gram_ref):
     width = 80
-    last = packets_ref[:, 8 * width :]
-    peak_row = jnp.max(last, axis=0, keepdims=True)
-    ratio = last / peak_row
+    component = iota((8, 128), 1) & (RANK - 1)
+    offset = jnp.where(component < 8, 0, jnp.where(component < 16, 32, jnp.where(component < 24, 56, 72)))
+    eighth = (component & 7) == 7
+    place = jnp.where(eighth, jnp.maximum(offset - 32, 0), 48 + offset + (component & 7))
+    peaks = []
+    for d in range(0, packets_ref.shape[0], 8):
+        first = take_lanes(packets_ref[d : d + 8, 384:512], jnp.full((8, 128), 96, jnp.int32))
+        rest = take_lanes(packets_ref[d : d + 8, 512:], place)
+        peaks.append(jnp.where(component == 7, first, rest))
+    peaks = jnp.concatenate(peaks, axis=0)
+    peak_row = jnp.max(peaks, axis=0, keepdims=True)
+    ratio = peaks / peak_row
     tiles = []
     for t in range(5):
         place = iota((8, 128), 1) + 128 * t
@@ -187,7 +199,7 @@
         axis=0,
     )
     row, column = iota((RANK, RANK), 0), iota((RANK, RANK), 1)
-    gram_ref[...] = jnp.where((row >> 3) <= (column >> 3), upper, upper.T)
+    gram_ref[...] = jnp.where(row <= column, upper, upper.T)
     peak_ref[...] = peak_row[:, :RANK]
     factor_ref[...] = raw_ref[...] / as_column(peak_row[:, :RANK])
 
@@ -243,10 +255,10 @@
     mine = (partial + one) + (two + three)
     other = shift(mine, "samp", 2, 1)
     (inverse,) = call(invert_kernel, [(RANK, RANK)], [VMEM], name="invert")(mine)
-    raw, packets = call(solve_kernel, [(RANK, 64), (RANK, 1, 768)], [VMEM] * 3, name="solve")(
+    raw, packets = call(solve_kernel, [(RANK, 64), (RANK, 1, 640)], [VMEM] * 3, name="solve")(
         mine, other, inverse
     )
-    packets = exchange(packets, 4, False).reshape(RANK, 768)
+    packets = exchange(packets, 4, False).reshape(RANK, 640)
     factor, peak, gram = call(
         finish_kernel, [(RANK, 64), (1, RANK), (RANK, RANK)], [VMEM] * 2, name="finish"
     )(packets, raw)

time: 44.7 us -> 44.2 us (0.989)
  blocking collectives: 26.8 us -> 26.3 us
    all_to_all x2, blocking collectives: 26.8 us -> 26.3 us  [exchange(): lax.all_to_all(x, ('mz', 'rt', 'samp'), 0, 0, axis_index_groups=groups)]
where the time goes in v7:
time: 44.2 us; the launch traced here: 44 us
  blocking collectives  26.3 us (60%)
  starting transfers between devices  8.28 us (19%)
  waiting for transfers between devices  4.44 us (10%)
  Pallas kernels  3.61 us (8%)
  other arithmetic  0.72 us (2%)
  between operations  0.66 us (1%)
    all_to_all x2, blocking collectives, exchange(): lax.all_to_all(x, ('mz', 'rt', 'samp'), 0, 0, axis_index_groups=groups)  26.3 us
    ppermute x3, waiting for transfers between devices, swap(): return lax.ppermute(x, ('rt', 'samp'), pairs)  4.32 us
    ppermute x2, starting transfers between devices, shift(): return lax.ppermute(x, axis, [(i, (i + by) % size) for i in range(size)])  4.2 us
    ppermute x3, starting transfers between devices, swap(): return lax.ppermute(x, ('rt', 'samp'), pairs)  4.07 us
    pallas_call x1, Pallas kernels, local(): call(finish_kernel, [(RANK, 64), (1, RANK), (RANK, RANK)], [VMEM] * 2, na...  1.1 us
    pallas_call x1, Pallas kernels, local(): call(contract_kernel, [(TILES * RANK + 8, 128)], [VMEM] * 2, name='contra...  1.03 us
  transfers between devices with their start and end apart: 5, of which 3 were waited for; matrix products, arithmetic and copies ran while one was open for 2% of the time, Pallas kernels for 2%

profile of v7, /device:TPU:1, one launch (start us, length us, event | category | flops | bytes accessed | tf_op | source)
XLA Modules:
  0.0 44.0 jit_solution(14029139298975954571)
XLA Ops:
  0.6 3.3 %collective-permute-start = (f32[4,512,512]{2,1,0:T(8,128)}, f32[4,512,512]{2,1,0:T(8,128)S(1)}, u32[]{:S(2)}, u32[]{:S(2)}) collective-permute-start(f32[4,512,512]{2,1,0:T(8,128)} %param.3), channel_id=1, source_target_pairs={{0,1},{1,0},{2,3},{3,2},{4,5},{5,4},{6,7},{7,6},{8,9},{9,8},{10,11... | collective-permute-start | bytes 12582920 | tf_op jit(solution)/shard_map/ppermute | solution.py:219
  4.0 0.7 %select_maximum_fusion.packet_ref = f32[8,128]{1,0:T(8,128)S(1)} fusion(f32[4,32]{1,0:T(4,128)} %bitcast.11, f32[4,128]{1,0:T(4,128)} %bitcast.12), kind=kLoop, calls=%fused_computation.3 | loop fusion | flops 3072 | bytes 6656 | tf_op jit(solution)/shard_map/concatenate | solution.py:247
  4.7 0.1 spread.1
  4.8 14.3 %all_to_all.10 = f32[32,1,640]{2,1,0:T(1,128)S(1)} all-to-all(f32[32,1,640]{2,1,0:T(1,128)S(1)} %spread.1), channel_id=1, replica_groups={{144,152,160,168,176,184,192,200,208,216,224,232,240,248,0,8,16,24,32,4..., dimensions={0} | all-to-all | bytes 163840 | tf_op jit(solution)/shard_map/all_to_all | solution.py:241
  19.0 0.0 collective-permute-done.spectra_ref
  19.0 1.0 %contract.1 = f32[136,128]{1,0:T(8,128)S(1)} custom-call(f32[4,512,512]{2,1,0:T(8,128)S(1)} %collective-permute-done.spectra_ref, f32[32,640]{1,0:T(8,128)S(1)} %bitcast.10), custom_call_target="tpu_custom_call" | custom-call | tf_op jit(solution)/shard_map/contract/pallas_call | solution.py:251
  20.1 2.5 %collective-permute-start.3 = (f32[136,128]{1,0:T(8,128)S(1)}, f32[136,128]{1,0:T(8,128)S(1)}, u32[]{:S(2)}, u32[]{:S(2)}) collective-permute-start(f32[136,128]{1,0:T(8,128)S(1)} %contract.1), channel_id=1, source_target_pairs={{0,6},{1,7},{2,4},{3,5},{4,2},{5,3},{6,0},{7,1},{8,14},{9,15},{10,... | collective-permute-start | bytes 208904 | tf_op jit(solution)/shard_map/ppermute | solution.py:224
  22.6 1.6 %collective-permute-start.2 = (f32[136,128]{1,0:T(8,128)S(1)}, f32[136,128]{1,0:T(8,128)S(1)}, u32[]{:S(2)}, u32[]{:S(2)}) collective-permute-start(f32[136,128]{1,0:T(8,128)S(1)} %contract.1), channel_id=1, source_target_pairs={{0,5},{1,4},{2,7},{3,6},{4,1},{5,0},{6,3},{7,2},{8,13},{9,12},{10,... | collective-permute-start | bytes 208904 | tf_op jit(solution)/shard_map/ppermute | solution.py:224
  24.1 0.0 collective-permute-start.1
  24.1 0.3 collective-permute-done.3
  24.5 4.0 %collective-permute-done.2 = f32[136,128]{1,0:T(8,128)S(1)} collective-permute-done((f32[136,128]{1,0:T(8,128)S(1)}, f32[136,128]{1,0:T(8,128)S(1)}, u32[]{:S(2)}, u32[]{:S(2)}) %collective-permute-start.2) | collective-permute-done | bytes 69664 | tf_op jit(solution)/shard_map/ppermute | solution.py:224
  28.5 0.0 collective-permute-done.1
  28.5 0.9 %collective-permute-start.4 = (f32[136,128]{1,0:T(8,128)S(1)}, f32[136,128]{1,0:T(8,128)S(1)}, u32[]{:S(2)}, u32[]{:S(2)}) collective-permute-start(f32[136,128]{1,0:T(8,128)S(1)} %add_add_fusion.total_ref.mine_ref), channel_id=1, source_target_pairs={{0,1},{1,0},{2,3},{3,2},{4,5},{5,4},{6,7},{7,6},{8,9},{9,8},{10,11... | collective-permute-start | bytes 208904 | tf_op jit(solution)/shard_map/ppermute | solution.py:219
  29.4 0.8 %invert.1.inverse_ref = f32[32,32]{1,0:T(8,128)S(1)} custom-call(f32[136,128]{1,0:T(8,128)S(1)} %add_add_fusion.total_ref.mine_ref), custom_call_target="tpu_custom_call" | custom-call | tf_op jit(solution)/shard_map/invert/pallas_call | solution.py:257
  30.2 0.1 collective-permute-done.4.other_ref
  30.3 0.6 %solve.1 = (f32[32,64]{1,0:T(8,128)S(1)}, f32[32,1,640]{2,1,0:T(1,128)S(1)}) custom-call(f32[136,128]{1,0:T(8,128)S(1)} %add_add_fusion.total_ref.mine_ref, f32[136,128]{1,0:T(8,128)S(1)} %collective-permute-done.4.other_ref, f32[32,32]{1,0:T(8,128)S(1)} %invert.1.inverse_ref), custom_call_target="tpu_custom_call" | custom-call | tf_op jit(solution)/shard_map/solve/pallas_call | solution.py:258
  30.9 12.0 %all_to_all.11 = f32[32,1,640]{2,1,0:T(1,128)S(1)} all-to-all(f32[32,1,640]{2,1,0:T(1,128)S(1)} %get-tuple-element.8), channel_id=1, replica_groups={{144,0,8,24,32,224,16,40,56,64,192,232,248,48,72,88,96,160,200,216,240,..., dimensions={0} | all-to-all | bytes 163840 | tf_op jit(solution)/shard_map/all_to_all | solution.py:241
  42.9 1.1 %finish.1 = (f32[32,64]{1,0:T(8,128)}, f32[1,32]{1,0:T(1,128)}, f32[32,32]{1,0:T(8,128)}) custom-call(f32[32,640]{1,0:T(8,128)S(1)} %bitcast.9, f32[32,64]{1,0:T(8,128)S(1)} %get-tuple-element.9.raw_ref), custom_call_target="tpu_custom_call" | custom-call | tf_op jit(solution)/shard_map/finish/pallas_call | solution.py:262
  (3 shorter events, 0.0 us)
Async XLA Ops:
  0.6 18.4 %collective-permute-start = (f32[4,512,512]{2,1,0:T(8,128)}, f32[4,512,512]{2,1,0:T(8,128)S(1)}, u32[]{:S(2)}, u32[]{:S(2)}) collective-permute-start(f32[4,512,512]{2,1,0:T(8,128)} %param.3), channel_id=1, source_target_pairs={{0,1},{1,0},{2,3},{3,2},{4,5},{5,4},{6,7},{7,6},{8,9},{9,8},{10,11... | collective-permute-start | bytes 12582920 | tf_op jit(solution)/shard_map/ppermute | solution.py:219
  20.1 4.4 %collective-permute-start.3 = (f32[136,128]{1,0:T(8,128)S(1)}, f32[136,128]{1,0:T(8,128)S(1)}, u32[]{:S(2)}, u32[]{:S(2)}) collective-permute-start(f32[136,128]{1,0:T(8,128)S(1)} %contract.1), channel_id=1, source_target_pairs={{0,6},{1,7},{2,4},{3,5},{4,2},{5,3},{6,0},{7,1},{8,14},{9,15},{10,... | collective-permute-start | bytes 208904 | tf_op jit(solution)/shard_map/ppermute | solution.py:224
  22.6 5.9 %collective-permute-start.2 = (f32[136,128]{1,0:T(8,128)S(1)}, f32[136,128]{1,0:T(8,128)S(1)}, u32[]{:S(2)}, u32[]{:S(2)}) collective-permute-start(f32[136,128]{1,0:T(8,128)S(1)} %contract.1), channel_id=1, source_target_pairs={{0,5},{1,4},{2,7},{3,6},{4,1},{5,0},{6,3},{7,2},{8,13},{9,12},{10,... | collective-permute-start | bytes 208904 | tf_op jit(solution)/shard_map/ppermute | solution.py:224
  24.1 4.3 %collective-permute-start.1 = (f32[136,128]{1,0:T(8,128)S(1)}, f32[136,128]{1,0:T(8,128)S(1)}, u32[]{:S(2)}, u32[]{:S(2)}) collective-permute-start(f32[136,128]{1,0:T(8,128)S(1)} %contract.1), channel_id=1, source_target_pairs={{0,3},{1,2},{2,1},{3,0},{4,7},{5,6},{6,5},{7,4},{8,11},{9,10},{10,... | collective-permute-start | bytes 208904 | tf_op jit(solution)/shard_map/ppermute | solution.py:224
  28.5 1.8 %collective-permute-start.4 = (f32[136,128]{1,0:T(8,128)S(1)}, f32[136,128]{1,0:T(8,128)S(1)}, u32[]{:S(2)}, u32[]{:S(2)}) collective-permute-start(f32[136,128]{1,0:T(8,128)S(1)} %add_add_fusion.total_ref.mine_ref), channel_id=1, source_target_pairs={{0,1},{1,0},{2,3},{3,2},{4,5},{5,4},{6,7},{7,6},{8,9},{9,8},{10,11... | collective-permute-start | bytes 208904 | tf_op jit(solution)/shard_map/ppermute | solution.py:219

commit v8 on v7

--- a/solution.py
+++ b/solution.py
@@ -49,8 +49,8 @@
     return [FIRST] + sorted([c for c in range(RANK) if c != FIRST], key=key)
 
 
-ORDER_A = [(FIRST + i) % RANK for i in range(RANK)]
-ORDER_C = ordered(lambda chip: dist(chip, 0))
+ORDER_A = ordered(lambda chip: dist(chip, 0))
+ORDER_C = ORDER_A
 
 
 def in_order(x):

time: 44.2 us -> 44.1 us (level)
  transfers between devices with their start and end apart: 5 -> 5, of which waited for: 3 -> 4; matrix products, arithmetic and copies ran while one was open for 2% -> 2% of each run, Pallas kernels for 2% -> 2%
where the time goes in v8:
time: 44.1 us; the launch traced here: 43.9 us
  blocking collectives  26.2 us (59%)
  starting transfers between devices  8.57 us (19%)
  waiting for transfers between devices  4.14 us (9%)
  Pallas kernels  3.6 us (8%)
  other arithmetic  0.72 us (2%)
  between operations  0.65 us (1%)
    all_to_all x2, blocking collectives, exchange(): lax.all_to_all(x, ('mz', 'rt', 'samp'), 0, 0, axis_index_groups=groups)  26.2 us
    ppermute x3, starting transfers between devices, swap(): return lax.ppermute(x, ('rt', 'samp'), pairs)  4.34 us
    ppermute x2, starting transfers between devices, shift(): return lax.ppermute(x, axis, [(i, (i + by) % size) for i in range(size)])  4.24 us
    ppermute x3, waiting for transfers between devices, swap(): return lax.ppermute(x, ('rt', 'samp'), pairs)  4.03 us
    pallas_call x1, Pallas kernels, local(): call(finish_kernel, [(RANK, 64), (1, RANK), (RANK, RANK)], [VMEM] * 2, na...  1.1 us
    pallas_call x1, Pallas kernels, local(): call(contract_kernel, [(TILES * RANK + 8, 128)], [VMEM] * 2, name='contra...  1.02 us
  transfers between devices with their start and end apart: 5, of which 4 were waited for; matrix products, arithmetic and copies ran while one was open for 2% of the time, Pallas kernels for 2%

profile of v8, /device:TPU:1, one launch (start us, length us, event | category | flops | bytes accessed | tf_op | source)
XLA Modules:
  0.0 43.9 jit_solution(13349896778142347274)
XLA Ops:
  0.6 3.3 %collective-permute-start = (f32[4,512,512]{2,1,0:T(8,128)}, f32[4,512,512]{2,1,0:T(8,128)S(1)}, u32[]{:S(2)}, u32[]{:S(2)}) collective-permute-start(f32[4,512,512]{2,1,0:T(8,128)} %param.3), channel_id=1, source_target_pairs={{0,1},{1,0},{2,3},{3,2},{4,5},{5,4},{6,7},{7,6},{8,9},{9,8},{10,11... | collective-permute-start | bytes 12582920 | tf_op jit(solution)/shard_map/ppermute | solution.py:219
  4.0 0.7 %select_maximum_fusion.packet_ref = f32[8,128]{1,0:T(8,128)S(1)} fusion(f32[4,32]{1,0:T(4,128)} %bitcast.11, f32[4,128]{1,0:T(4,128)} %bitcast.12), kind=kLoop, calls=%fused_computation.3 | loop fusion | flops 3072 | bytes 6656 | tf_op jit(solution)/shard_map/concatenate | solution.py:247
  4.7 0.1 spread.1
  4.8 13.9 %all_to_all.10 = f32[32,1,640]{2,1,0:T(1,128)S(1)} all-to-all(f32[32,1,640]{2,1,0:T(1,128)S(1)} %spread.1), channel_id=1, replica_groups={{144,0,8,24,32,224,16,40,56,64,192,232,248,48,72,88,96,160,200,216,240,..., dimensions={0} | all-to-all | bytes 163840 | tf_op jit(solution)/shard_map/all_to_all | solution.py:241
  18.7 0.0 collective-permute-done.spectra_ref
  18.7 1.0 %contract.1 = f32[136,128]{1,0:T(8,128)S(1)} custom-call(f32[4,512,512]{2,1,0:T(8,128)S(1)} %collective-permute-done.spectra_ref, f32[32,640]{1,0:T(8,128)S(1)} %bitcast.10), custom_call_target="tpu_custom_call" | custom-call | tf_op jit(solution)/shard_map/contract/pallas_call | solution.py:251
  19.7 2.5 %collective-permute-start.3 = (f32[136,128]{1,0:T(8,128)S(1)}, f32[136,128]{1,0:T(8,128)S(1)}, u32[]{:S(2)}, u32[]{:S(2)}) collective-permute-start(f32[136,128]{1,0:T(8,128)S(1)} %contract.1), channel_id=1, source_target_pairs={{0,6},{1,7},{2,4},{3,5},{4,2},{5,3},{6,0},{7,1},{8,14},{9,15},{10,... | collective-permute-start | bytes 208904 | tf_op jit(solution)/shard_map/ppermute | solution.py:224
  22.2 1.8 %collective-permute-start.2 = (f32[136,128]{1,0:T(8,128)S(1)}, f32[136,128]{1,0:T(8,128)S(1)}, u32[]{:S(2)}, u32[]{:S(2)}) collective-permute-start(f32[136,128]{1,0:T(8,128)S(1)} %contract.1), channel_id=1, source_target_pairs={{0,5},{1,4},{2,7},{3,6},{4,1},{5,0},{6,3},{7,2},{8,13},{9,12},{10,... | collective-permute-start | bytes 208904 | tf_op jit(solution)/shard_map/ppermute | solution.py:224
  24.0 0.0 collective-permute-start.1
  24.1 0.1 collective-permute-done.3
  24.1 3.7 %collective-permute-done.2 = f32[136,128]{1,0:T(8,128)S(1)} collective-permute-done((f32[136,128]{1,0:T(8,128)S(1)}, f32[136,128]{1,0:T(8,128)S(1)}, u32[]{:S(2)}, u32[]{:S(2)}) %collective-permute-start.2) | collective-permute-done | bytes 69664 | tf_op jit(solution)/shard_map/ppermute | solution.py:224
  27.8 0.3 collective-permute-done.1
  28.1 0.9 %collective-permute-start.4 = (f32[136,128]{1,0:T(8,128)S(1)}, f32[136,128]{1,0:T(8,128)S(1)}, u32[]{:S(2)}, u32[]{:S(2)}) collective-permute-start(f32[136,128]{1,0:T(8,128)S(1)} %add_add_fusion.total_ref.mine_ref), channel_id=1, source_target_pairs={{0,1},{1,0},{2,3},{3,2},{4,5},{5,4},{6,7},{7,6},{8,9},{9,8},{10,11... | collective-permute-start | bytes 208904 | tf_op jit(solution)/shard_map/ppermute | solution.py:219
  29.0 0.8 %invert.1.inverse_ref = f32[32,32]{1,0:T(8,128)S(1)} custom-call(f32[136,128]{1,0:T(8,128)S(1)} %add_add_fusion.total_ref.mine_ref), custom_call_target="tpu_custom_call" | custom-call | tf_op jit(solution)/shard_map/invert/pallas_call | solution.py:257
  29.8 0.1 collective-permute-done.4.other_ref
  29.9 0.6 %solve.1 = (f32[32,64]{1,0:T(8,128)S(1)}, f32[32,1,640]{2,1,0:T(1,128)S(1)}) custom-call(f32[136,128]{1,0:T(8,128)S(1)} %add_add_fusion.total_ref.mine_ref, f32[136,128]{1,0:T(8,128)S(1)} %collective-permute-done.4.other_ref, f32[32,32]{1,0:T(8,128)S(1)} %invert.1.inverse_ref), custom_call_target="tpu_custom_call" | custom-call | tf_op jit(solution)/shard_map/solve/pallas_call | solution.py:258
  30.5 12.3 %all_to_all.11 = f32[32,1,640]{2,1,0:T(1,128)S(1)} all-to-all(f32[32,1,640]{2,1,0:T(1,128)S(1)} %get-tuple-element.8), channel_id=1, replica_groups={{144,0,8,24,32,224,16,40,56,64,192,232,248,48,72,88,96,160,200,216,240,..., dimensions={0} | all-to-all | bytes 163840 | tf_op jit(solution)/shard_map/all_to_all | solution.py:241
  42.8 1.1 %finish.1 = (f32[32,64]{1,0:T(8,128)}, f32[1,32]{1,0:T(1,128)}, f32[32,32]{1,0:T(8,128)}) custom-call(f32[32,640]{1,0:T(8,128)S(1)} %bitcast.9, f32[32,64]{1,0:T(8,128)S(1)} %get-tuple-element.9.raw_ref), custom_call_target="tpu_custom_call" | custom-call | tf_op jit(solution)/shard_map/finish/pallas_call | solution.py:262
  (3 shorter events, 0.0 us)
Async XLA Ops:
  0.6 18.1 %collective-permute-start = (f32[4,512,512]{2,1,0:T(8,128)}, f32[4,512,512]{2,1,0:T(8,128)S(1)}, u32[]{:S(2)}, u32[]{:S(2)}) collective-permute-start(f32[4,512,512]{2,1,0:T(8,128)} %param.3), channel_id=1, source_target_pairs={{0,1},{1,0},{2,3},{3,2},{4,5},{5,4},{6,7},{7,6},{8,9},{9,8},{10,11... | collective-permute-start | bytes 12582920 | tf_op jit(solution)/shard_map/ppermute | solution.py:219
  19.7 4.4 %collective-permute-start.3 = (f32[136,128]{1,0:T(8,128)S(1)}, f32[136,128]{1,0:T(8,128)S(1)}, u32[]{:S(2)}, u32[]{:S(2)}) collective-permute-start(f32[136,128]{1,0:T(8,128)S(1)} %contract.1), channel_id=1, source_target_pairs={{0,6},{1,7},{2,4},{3,5},{4,2},{5,3},{6,0},{7,1},{8,14},{9,15},{10,... | collective-permute-start | bytes 208904 | tf_op jit(solution)/shard_map/ppermute | solution.py:224
  22.2 5.6 %collective-permute-start.2 = (f32[136,128]{1,0:T(8,128)S(1)}, f32[136,128]{1,0:T(8,128)S(1)}, u32[]{:S(2)}, u32[]{:S(2)}) collective-permute-start(f32[136,128]{1,0:T(8,128)S(1)} %contract.1), channel_id=1, source_target_pairs={{0,5},{1,4},{2,7},{3,6},{4,1},{5,0},{6,3},{7,2},{8,13},{9,12},{10,... | collective-permute-start | bytes 208904 | tf_op jit(solution)/shard_map/ppermute | solution.py:224
  24.0 4.0 %collective-permute-start.1 = (f32[136,128]{1,0:T(8,128)S(1)}, f32[136,128]{1,0:T(8,128)S(1)}, u32[]{:S(2)}, u32[]{:S(2)}) collective-permute-start(f32[136,128]{1,0:T(8,128)S(1)} %contract.1), channel_id=1, source_target_pairs={{0,3},{1,2},{2,1},{3,0},{4,7},{5,6},{6,5},{7,4},{8,11},{9,10},{10,... | collective-permute-start | bytes 208904 | tf_op jit(solution)/shard_map/ppermute | solution.py:224
  28.1 1.8 %collective-permute-start.4 = (f32[136,128]{1,0:T(8,128)S(1)}, f32[136,128]{1,0:T(8,128)S(1)}, u32[]{:S(2)}, u32[]{:S(2)}) collective-permute-start(f32[136,128]{1,0:T(8,128)S(1)} %add_add_fusion.total_ref.mine_ref), channel_id=1, source_target_pairs={{0,1},{1,0},{2,3},{3,2},{4,5},{5,4},{6,7},{7,6},{8,9},{9,8},{10,11... | collective-permute-start | bytes 208904 | tf_op jit(solution)/shard_map/ppermute | solution.py:219
